TPU v7x, 32 devices: a whole 2x2x4 slice. The times are simulated.
32 devices in a mesh: group: 2 (over y), gx: 4 (over z), gy: 2 (over x), gz: 2 (over core).
Axes of the slice: x: 2, y: 2, z: 4, core: 2. Of those that a mesh axis runs over, the one named last changes fastest.
Arguments:
- base_state: float32 [16, 8, 384, 256], P('group', 'gz', 'gx', 'gy'), parts along dimension 0, may hold values from -6 to 6
- tendency: bfloat16 [16, 8, 384, 256], P('group', 'gz', 'gx', 'gy'), parts along dimension 0, may hold values from -6 to 6
- inflow: float32 [4, 18432], P('group', ('gx', 'gy')), parts along dimension 0, may hold values from 0.5 to 2
- chord_len: float32 [36864], P(('group', 'gx', 'gy')), parts along dimension 0, may hold values from 2 to 6
- twist_base: float32 [36864], P(('group', 'gx', 'gy')), parts along dimension 0, may hold values from 0 to 0.4
- compliance: float32 [36864], P(('group', 'gx', 'gy')), parts along dimension 0, may hold values from 0.005 to 0.05
- blade_frame: float32 [32, 18432], P('group', ('gx', 'gy')), parts along dimension 0, may hold values from -6 to 6
- owner_tile: int32 [18432, 2], P(('gx', 'gy'), 'group'), parts along dimension 1, may hold values from 0 to 7; in each aligned block of 2304 rows (0 to 2303, 2304 to 4607, ...) at most 576 rows name the same one
- point_cells: int32 [6, 18432], P('group', ('gx', 'gy')), parts along dimension 0, may hold values from 0 to 127, as said below
Outputs:
- forced_state: float32 [16, 8, 384, 256], P('group', 'gz', 'gx', 'gy'), parts along dimension 0
- divergence_lines: float32 [16, 256, 384], P(('group', 'gz'), ('gy', 'gx')), parts along dimension 0
There are 2 independent parts, one for each index of `group`. A program takes and returns all parts, laid end to end along the dimension named above; each array names one. Nothing has to cross between parts.
Inputs may be any that keep to these rules, and one draw needn't show every extreme that they name: `owner_tile`: within the points of one device (aligned blocks of 2304 points), no tile is named by more than 576 points, a bound that some block reaches. `point_cells`: row 0 is the x cell within the owning tile (below 96), row 1 the y cell within it (below 128), row 2 the global z level (below 8).
All inputs are finite; a program needn't handle non-finite values.
Results may differ from a plain program's by a relative error of at most 0.00056.
Values sent between devices are 32-bit elements; how exact they have to be, the bound alone decides.
A program may use at most 64 MiB of HBM per device.

v0:
```python
import math

import jax
import jax.numpy as jnp
from jax import lax
from jax.sharding import PartitionSpec as P

sigma_xy = 3.0
sigma_z = 1.5
reach_cells = 8
tap_total = sum([math.exp(-((float(offset_cell) / sigma_xy) ** 2)) for offset_cell in range(-8, 9)])


def padded_2(cells, sides, width):
    for axis, dim in sides:
        count = lax.axis_size(axis)
        ends = count - 1
        head = lax.slice_in_dim(cells, 0, width, axis=dim)
        tail = lax.slice_in_dim(cells, cells.shape[dim] - width, cells.shape[dim], axis=dim)
        cells = jnp.concatenate(
            [
                lax.ppermute(tail, axis, [(i, (i + 1) % count) for i in range(ends)]),
                cells,
                lax.ppermute(head, axis, [((i + 1) % count, i) for i in range(ends)]),
            ],
            axis=dim,
        )
    return cells


def tap_weight(offset):
    scaled = offset.astype(jnp.float32) / sigma_xy
    return jnp.where(jnp.abs(offset) <= reach_cells, jnp.exp(-scaled * scaled) / tap_total, 0.0)


def point_forces(inflow, chord_len, twist_base, compliance, blade_frame):
    normal = inflow[0]
    tangent = inflow[1]
    speed_sq = normal * normal + tangent * tangent
    twist_angle = twist_base + compliance * speed_sq
    attack = jnp.arctan2(normal, tangent) - twist_angle
    pressure = 0.5 * speed_sq * chord_len
    lift_force = pressure * (2.0 * math.pi) * jnp.sin(attack)
    drag_force = pressure * (0.01 + 0.5 * attack * attack)
    half = blade_frame.shape[0] // 2
    return blade_frame[:half] * lift_force[None, :] + blade_frame[half:] * drag_force[None, :]


def pack_points(forces, point_cells, owners, tiles, capacity):
    points_here = owners.shape[0]
    onehot = (owners[:, None] == jnp.arange(tiles, dtype=jnp.int32)[None, :]).astype(jnp.int32)
    counts = jnp.sum(onehot, axis=0)
    starts = jnp.cumsum(counts) - counts
    order = jnp.argsort(owners, stable=True)
    position = jnp.arange(tiles * capacity, dtype=jnp.int32) % capacity
    live = position < jnp.repeat(counts, capacity)
    source_row = jnp.minimum(jnp.repeat(starts, capacity) + position, points_here - 1)
    chosen = order[source_row]
    force_rows = jnp.where(live[None, :], forces[:, chosen], 0.0)
    cell_rows = jnp.where(live[None, :], point_cells[:, chosen], 0)
    return (force_rows, cell_rows)


def smear_tile(force_rows, cell_rows, first_level, levels_here, levels_all, width_x, width_y):
    x_local = cell_rows[0]
    y_local = cell_rows[1]
    z_global = cell_rows[2]
    columns_x = jnp.arange(width_x + 16, dtype=jnp.int32) - reach_cells
    columns_y = jnp.arange(width_y + 16, dtype=jnp.int32) - reach_cells
    weight_x = tap_weight(columns_x[None, :] - x_local[:, None])
    weight_y = tap_weight(columns_y[None, :] - y_local[:, None]).astype(jnp.bfloat16)
    every_level = jnp.arange(levels_all, dtype=jnp.int32)
    spread_all = (every_level[None, :] - z_global[:, None]).astype(jnp.float32) / sigma_z
    level_total = jnp.sum(jnp.exp(-spread_all * spread_all), axis=1)
    own_levels = first_level + jnp.arange(levels_here, dtype=jnp.int32)
    spread_own = (own_levels[None, :] - z_global[:, None]).astype(jnp.float32) / sigma_z
    weight_z = jnp.exp(-spread_own * spread_own) / level_total[:, None]
    planes = []
    for channel in range(force_rows.shape[0]):
        weighted = (
            (force_rows[channel][:, None] * weight_z)[:, :, None] * weight_x[:, None, :]
        ).astype(jnp.bfloat16)
        weighted = weighted.reshape(weighted.shape[0], levels_here * (width_x + 16))
        plane = lax.dot_general(
            weighted, weight_y, (((0,), (0,)), ((), ())), preferred_element_type=jnp.float32
        )
        planes.append(plane.reshape(levels_here, width_x + 16, width_y + 16))
    return jnp.stack(planes)


def spread_rims(padded):
    spill_x = jnp.concatenate([padded[:, :, :8], padded[:, :, -8:]], axis=2)
    arrived_x = padded_2(spill_x, (("gx", 2),), 8)
    interior = padded[:, :, 8:-8]
    interior = jnp.concatenate(
        [
            interior[:, :, :8] + arrived_x[:, :, :8],
            interior[:, :, 8:-8],
            interior[:, :, -8:] + arrived_x[:, :, -8:],
        ],
        axis=2,
    )
    spill_y = jnp.concatenate([interior[:, :, :, :8], interior[:, :, :, -8:]], axis=3)
    arrived_y = padded_2(spill_y, (("gy", 3),), 8)
    interior = interior[:, :, :, 8:-8]
    interior = jnp.concatenate(
        [
            interior[:, :, :, :8] + arrived_y[:, :, :, :8],
            interior[:, :, :, 8:-8],
            interior[:, :, :, -8:] + arrived_y[:, :, :, -8:],
        ],
        axis=3,
    )
    return interior


def body(
    base_state,
    tendency,
    inflow,
    chord_len,
    twist_base,
    compliance,
    blade_frame,
    owner_tile,
    point_cells,
):
    tiles_x = lax.axis_size("gx")
    tiles_y = lax.axis_size("gy")
    tiles = tiles_x * tiles_y
    points_here = owner_tile.shape[0]
    capacity = max(2, (2 * points_here + tiles - 1) // tiles)
    forces = point_forces(inflow, chord_len, twist_base, compliance, blade_frame)
    force_rows, cell_rows = pack_points(forces, point_cells, owner_tile[:, 0], tiles, capacity)
    arrived_force, arrived_cells = (
        lax.all_to_all(force_rows, ("gx", "gy"), split_axis=1, concat_axis=1, tiled=True),
        lax.all_to_all(cell_rows, ("gx", "gy"), split_axis=1, concat_axis=1, tiled=True),
    )
    levels_here = base_state.shape[1]
    width_x = base_state.shape[2]
    width_y = base_state.shape[3]
    first_level = lax.axis_index("gz") * levels_here
    padded = smear_tile(
        arrived_force,
        arrived_cells,
        first_level,
        levels_here,
        levels_here * lax.axis_size("gz"),
        width_x,
        width_y,
    )
    source = spread_rims(padded)
    forced_state = base_state + 0.5 * (tendency.astype(jnp.float32) + source)
    u_padded = padded_2(forced_state[0], (("gx", 1),), 1)
    v_padded = padded_2(forced_state[1], (("gy", 2),), 1)
    w_padded = padded_2(forced_state[2], (("gz", 0),), 1)
    along_x = u_padded[:, 2:, :] - u_padded[:, :-2, :]
    along_y = v_padded[:, :, 2:] - v_padded[:, :, :-2]
    along_z = w_padded[2:, :, :] - w_padded[:-2, :, :]
    divergence = 0.5 * (along_x + along_y + along_z)
    lines = jnp.transpose(divergence, (0, 2, 1))
    divergence_lines = lax.all_to_all(lines, "gx", split_axis=1, concat_axis=2, tiled=True)
    return (forced_state, divergence_lines)


def solution(mesh):
    in_specs = (
        P("group", "gz", "gx", "gy"),
        P("group", "gz", "gx", "gy"),
        P("group", ("gx", "gy")),
        P(("group", "gx", "gy")),
        P(("group", "gx", "gy")),
        P(("group", "gx", "gy")),
        P("group", ("gx", "gy")),
        P(("gx", "gy"), "group"),
        P("group", ("gx", "gy")),
    )
    out_specs = (P("group", "gz", "gx", "gy"), P(("group", "gz"), ("gy", "gx"), None))
    return jax.shard_map(body, mesh=mesh, in_specs=in_specs, out_specs=out_specs, check_vma=False)
```

profile of v0, /device:TPU:0, one launch (start us, length us, event | category | flops | bytes accessed | tf_op | source)
XLA Modules:
  0.0 176.4 jit_solution(670845826570481275)
XLA Ops:
  2.7 5.8 %sort.17 = (s32[2304]{0:T(1024)}, s32[2304]{0:T(1024)S(1)}) sort(s32[2304]{0:T(1024)S(1)} %reduce, s32[2304]{0:T(1024)S(1)} %iota.48), dimensions={0}, to_apply=%region_1.0 | sort | flops 27648 | bytes 36864 | tf_op jit(solution)/shard_map/jit(argsort)/sort | solution.py:54
  8.4 24.1 %gather_fusion = s32[4608]{0:T(1024)S(1)} fusion(s32[2304]{0:T(1024)S(1)} %get-tuple-element.3, s32[5120]{0:T(1024)S(1)} %pad_clamp_fusion.1), kind=kCustom, calls=%fused_computation | custom fusion | bytes 55296 | tf_op jit(solution)/shard_map/gather | solution.py:58
  33.6 8.5 %gather_fusion.2 = s32[4608,3]{1,0:T(8,128)S(1)} fusion(s32[3,2304]{0,1:T(8,128)S(1)} %copy.62, s32[5120]{0:T(1024)} %pad_clamp_fusion), kind=kCustom, calls=%fused_computation.2 | custom fusion | bytes 129024 | tf_op jit(solution)/shard_map/gather | solution.py:60
  43.6 7.3 %all-to-all-start.1 = ((s32[3,8,576]{2,0,1:T(4,128)}), s32[3,8,576]{2,0,1:T(4,128)}, u32[]{:S(2)}, u32[]{:S(2)}) async-start(s32[3,8,576]{2,0,1:T(4,128)} %broadcast_select_fusion.1), calls=%async_computation.1 | async-start | bytes 163840 | tf_op jit(solution)/shard_map/all_to_all | solution.py:137
  52.2 8.5 %gather_fusion.1 = f32[4608,8]{1,0:T(8,128)S(1)} fusion(f32[8,2304]{0,1:T(8,128)S(1)} %copy.60, s32[5120]{0:T(1024)} %pad_clamp_fusion), kind=kCustom, calls=%fused_computation.1 | custom fusion | bytes 313344 | tf_op jit(solution)/shard_map/gather | solution.py:59
  62.1 6.0 %all-to-all-start = ((f32[8,8,576]{2,0,1:T(8,128)}), f32[8,8,576]{2,0,1:T(8,128)S(1)}, u32[]{:S(2)}, u32[]{:S(2)}) async-start(f32[8,8,576]{2,0,1:T(8,128)} %broadcast_select_fusion), calls=%async_computation | async-start | bytes 327680 | tf_op jit(solution)/shard_map/all_to_all | solution.py:136
  69.3 2.3 %fusion.52 = f32[4608,112]{0,1:T(8,128)} fusion(s32[4608]{0:T(1024)S(1)} %sub.121, s32[112]{0:T(128)S(1)} %iota_add_fusion.1), kind=kLoop, calls=%fused_computation.65 | loop fusion | flops 4644864 | bytes 2083264 | tf_op jit(solution)/shard_map/jit(_where)/select_n | solution.py:33
  71.8 3.8 %all-to-all-done = f32[8,8,576]{2,0,1:T(8,128)S(1)} async-done(((f32[8,8,576]{2,0,1:T(8,128)}), f32[8,8,576]{2,0,1:T(8,128)S(1)}, u32[]{:S(2)}, u32[]{:S(2)}) %all-to-all-start) | async-done | bytes 147488 | tf_op jit(solution)/shard_map/all_to_all | solution.py:136
  76.9 3.5 %fusion.161 = f32[8,4,112,144]{2,3,1,0:T(8,128)S(1)} fusion(s32[4608]{0:T(1024)S(1)} %sub.126, s32[144]{0:T(256)S(1)} %copy-done.15, f32[4608,112]{0,1:T(8,128)} %fusion.52, f32[4608,4]{0,1:T(4,128)S(1)} %get-tuple-element.49), kind=kOutput, calls=%fused_computation.106 | convolution fusion | flops 605306880 | bytes 2452032 | tf_op jit(solution)/shard_map/dot_general | solution.py:84
  80.4 1.8 %fusion.151 = f32[8,4,112,144]{2,3,1,0:T(8,128)S(1)} fusion(f32[8,4,112,144]{2,3,1,0:T(8,128)S(1)} %fusion.161, s32[4608]{0:T(1024)S(1)} %sub.126, s32[144]{0:T(256)S(1)} %copy-done.15, f32[4608,4]{0,1:T(4,128)S(1)} %get-tuple-element.43, f32[4608,112]{0,1:T(8,128)S(1)} %copy-done.6), kind=kOutput, calls=%fused_computation.104 | convolution fusion | flops 605306880 | bytes 2454528 | tf_op jit(solution)/shard_map/dot_general | solution.py:84
  82.2 1.8 %fusion.141 = f32[8,4,112,144]{2,3,1,0:T(8,128)S(1)} fusion(f32[8,4,112,144]{2,3,1,0:T(8,128)S(1)} %fusion.151, s32[4608]{0:T(1024)S(1)} %sub.126, s32[144]{0:T(256)S(1)} %copy-done.15, f32[4608,4]{0,1:T(4,128)S(1)} %get-tuple-element.44, f32[4608,112]{0,1:T(8,128)S(1)} %copy-done.6), kind=kOutput, calls=%fused_computation.102 | convolution fusion | flops 605306880 | bytes 2454528 | tf_op jit(solution)/shard_map/dot_general | solution.py:84
  85.7 1.8 %fusion.121 = f32[8,4,112,144]{2,3,1,0:T(8,128)S(1)} fusion(f32[8,4,112,144]{2,3,1,0:T(8,128)S(1)} %fusion.131, s32[4608]{0:T(1024)S(1)} %sub.126, s32[144]{0:T(256)S(1)} %copy-done.15, f32[4608,4]{0,1:T(4,128)S(1)} %get-tuple-element.46, f32[4608,112]{0,1:T(8,128)S(1)} %copy-done.6), kind=kOutput, calls=%fused_computation.98 | convolution fusion | flops 605306880 | bytes 2454528 | tf_op jit(solution)/shard_map/dot_general | solution.py:84
  89.2 2.0 %fusion.101 = f32[8,4,112,144]{2,3,1,0:T(8,128)S(1)} fusion(f32[8,4,112,144]{2,3,1,0:T(8,128)S(1)} %fusion.111, s32[4608]{0:T(1024)S(1)} %sub.126, s32[144]{0:T(256)S(1)} %copy-done.15, f32[4608,4]{0,1:T(4,128)S(1)} %get-tuple-element.48, f32[4608,112]{0,1:T(8,128)S(1)} %copy-done.6), kind=kOutput, calls=%fused_computation.94 | convolution fusion | flops 605306880 | bytes 2454528 | tf_op jit(solution)/shard_map/dot_general | solution.py:84
  93.0 2.1 %slice.213 = f32[8,4,8,144]{2,3,1,0:T(8,128)} slice(f32[8,4,112,144]{2,3,1,0:T(8,128)S(1)} %fusion.91), slice={[0:8], [0:4], [104:112], [0:144]} | slice | bytes 294912 | tf_op jit(solution)/shard_map/slice | solution.py:92
  95.1 2.8 %copy.64 = f32[8,4,8,144]{3,2,1,0:T(8,128)S(1)} copy(f32[8,4,8,144]{2,3,1,0:T(8,128)} %slice.213) | data formatting | bytes 294912 | tf_op jit(solution)/shard_map/slice | solution.py:92
  97.9 1.8 %collective-permute-start = (f32[8,4,8,144]{3,2,1,0:T(8,128)S(1)}, f32[8,4,8,144]{3,2,1,0:T(8,128)S(1)}, u32[]{:S(2)}, u32[]{:S(2)}) collective-permute-start(f32[8,4,8,144]{3,2,1,0:T(8,128)S(1)} %copy.64), channel_id=1, source_target_pairs={{0,4},{4,8},{8,12},{1,5},{5,9},{9,13},{2,6},{6,10},{10,14},{3,7},{... | collective-permute-start | bytes 442376 | tf_op jit(solution)/shard_map/ppermute | solution.py:22
  99.7 3.9 %collective-permute-done = f32[8,4,8,144]{3,2,1,0:T(8,128)S(1)} collective-permute-done((f32[8,4,8,144]{3,2,1,0:T(8,128)S(1)}, f32[8,4,8,144]{3,2,1,0:T(8,128)S(1)}, u32[]{:S(2)}, u32[]{:S(2)}) %collective-permute-start) | collective-permute-done | bytes 147488 | tf_op jit(solution)/shard_map/ppermute | solution.py:22
  103.6 2.2 %copy.65 = f32[8,4,8,144]{2,3,1,0:T(8,128)} copy(f32[8,4,8,144]{3,2,1,0:T(8,128)S(1)} %collective-permute-done) | data formatting | bytes 294912 | tf_op jit(solution)/shard_map/ppermute | solution.py:22
  105.7 4.7 %slice_add_fusion.1 = (f32[8,4,8,144]{2,3,1,0:T(8,128)}, f32[8,4,8,144]{2,3,1,0:T(8,128)}) fusion(f32[8,4,8,144]{2,3,1,0:T(8,128)} %copy.65, f32[8,4,112,144]{2,3,1,0:T(8,128)S(1)} %fusion.91), kind=kLoop, calls=%fused_computation.56 | loop fusion | flops 36864 | bytes 737280 | tf_op jit(solution)/shard_map/add | solution.py:97
  110.4 2.8 %copy.66 = f32[8,4,8,144]{3,2,1,0:T(8,128)S(1)} copy(f32[8,4,8,144]{2,3,1,0:T(8,128)} %get-tuple-element.32) | data formatting | bytes 294912 | tf_op jit(solution)/shard_map/slice | solution.py:92
  114.5 2.3 %slice.214 = f32[8,4,80,144]{2,3,1,0:T(8,128)S(1)} slice(f32[8,4,112,144]{2,3,1,0:T(8,128)} %copy-done.4), slice={[0:8], [0:4], [16:96], [0:144]} | slice | bytes 2949120 | tf_op jit(solution)/shard_map/slice | solution.py:98
  116.8 5.1 %collective-permute-done.1 = f32[8,4,8,144]{3,2,1,0:T(8,128)S(1)} collective-permute-done((f32[8,4,8,144]{3,2,1,0:T(8,128)S(1)}, f32[8,4,8,144]{3,2,1,0:T(8,128)S(1)}, u32[]{:S(2)}, u32[]{:S(2)}) %collective-permute-start.1) | collective-permute-done | bytes 147488 | tf_op jit(solution)/shard_map/ppermute | solution.py:24
  121.9 2.2 %copy.67 = f32[8,4,8,144]{2,3,1,0:T(8,128)} copy(f32[8,4,8,144]{3,2,1,0:T(8,128)S(1)} %collective-permute-done.1) | data formatting | bytes 294912 | tf_op jit(solution)/shard_map/ppermute | solution.py:24
  124.1 3.2 %slice_add_fusion = f32[8,4,8,144]{2,3,1,0:T(8,128)S(1)} fusion(f32[8,4,8,144]{2,3,1,0:T(8,128)} %copy.67, f32[8,4,112,144]{2,3,1,0:T(8,128)} %copy-done.4), kind=kLoop, calls=%fused_computation.55 | loop fusion | flops 36864 | bytes 442368 | tf_op jit(solution)/shard_map/add | solution.py:99
  128.8 3.4 %collective-permute-start.2 = (f32[8,4,96,8]{2,3,1,0:T(8,128)}, f32[8,4,96,8]{2,3,1,0:T(8,128)S(1)}, u32[]{:S(2)}, u32[]{:S(2)}) collective-permute-start(f32[8,4,96,8]{2,3,1,0:T(8,128)} %pad_maximum_fusion.8), channel_id=1, source_target_pairs={{0,2},{1,3},{4,6},{5,7},{8,10},{9,11},{12,14},{13,15},{16,18},{17,... | collective-permute-start | bytes 294920 | tf_op jit(solution)/shard_map/ppermute | solution.py:22
  132.1 2.9 %copy.68 = f32[8,4,96,128]{2,3,1,0:T(8,128)} copy(f32[8,4,96,128]{3,2,1,0:T(8,128)} %param.9) | data formatting | bytes 3145728 | tf_op args[0]
  141.0 4.1 %collective-permute-done.3 = f32[8,4,96,8]{2,3,1,0:T(8,128)S(1)} collective-permute-done((f32[8,4,96,8]{2,3,1,0:T(8,128)S(1)}, f32[8,4,96,8]{2,3,1,0:T(8,128)S(1)}, u32[]{:S(2)}, u32[]{:S(2)}) %collective-permute-start.3) | collective-permute-done | bytes 98336 | tf_op jit(solution)/shard_map/ppermute | solution.py:24
  148.4 3.0 %collective-permute-start.9 = (f32[1,96,128]{1,2,0:T(8,128)S(1)}, f32[1,96,128]{1,2,0:T(8,128)S(1)}, u32[]{:S(2)}, u32[]{:S(2)}) collective-permute-start(f32[1,96,128]{1,2,0:T(8,128)S(1)} %get-tuple-element.37), channel_id=1, source_target_pairs={{0,1},{2,3},{4,5},{6,7},{8,9},{10,11},{12,13},{14,15},{16,17},{18,... | collective-permute-start | bytes 147464 | tf_op jit(solution)/shard_map/ppermute | solution.py:22
  152.9 4.6 %collective-permute-start.5 = (f32[4,1,128]{1,2,0:T(8,128)S(1)}, f32[4,1,128]{1,2,0:T(8,128)S(1)}, u32[]{:S(2)}, u32[]{:S(2)}) collective-permute-start(f32[4,1,128]{1,2,0:T(8,128)S(1)} %get-tuple-element.39), channel_id=1, source_target_pairs={{0,4},{4,8},{8,12},{1,5},{5,9},{9,13},{2,6},{6,10},{10,14},{3,7},{... | collective-permute-start | bytes 6152 | tf_op jit(solution)/shard_map/ppermute | solution.py:22
  157.4 4.5 %collective-permute-start.7 = (f32[4,96,1]{1,2,0:T(1,128)S(1)}, f32[4,96,1]{1,2,0:T(1,128)S(1)}, u32[]{:S(2)}, u32[]{:S(2)}) collective-permute-start(f32[4,96,1]{1,2,0:T(1,128)S(1)} %get-tuple-element.41), channel_id=1, source_target_pairs={{0,2},{1,3},{4,6},{5,7},{8,10},{9,11},{12,14},{13,15},{16,18},{17,... | collective-permute-start | bytes 4616 | tf_op jit(solution)/shard_map/ppermute | solution.py:22
  164.5 4.1 %all-to-all-start.2 = ((f32[4,128,96]{2,0,1:T(4,128)}), f32[4,128,96]{2,0,1:T(4,128)S(1)}, u32[]{:S(2)}, u32[]{:S(2)}) async-start(f32[4,128,96]{2,0,1:T(4,128)} %copy.69), calls=%async_computation.2 | async-start | bytes 524288 | tf_op jit(solution)/shard_map/all_to_all | solution.py:162
  170.3 5.1 %all-to-all-done.2 = f32[4,128,96]{2,0,1:T(4,128)S(1)} async-done(((f32[4,128,96]{2,0,1:T(4,128)}), f32[4,128,96]{2,0,1:T(4,128)S(1)}, u32[]{:S(2)}, u32[]{:S(2)}) %all-to-all-start.2) | async-done | bytes 196640 | tf_op jit(solution)/shard_map/all_to_all | solution.py:162
  (104 shorter events, 33.7 us)
Async XLA Ops:
  8.4 24.8 %copy-start.11 = (s32[3,2304]{1,0:T(4,128)S(1)}, s32[3,2304]{1,0:T(4,128)}, u32[]{:S(2)}) copy-start(s32[3,2304]{1,0:T(4,128)} %param.17) | copy-start | bytes 82948
  33.2 18.4 %copy-start.8 = (f32[2304]{0:T(1024)S(1)}, f32[2304]{0:T(1024)}, u32[]{:S(2)}) copy-start(f32[2304]{0:T(1024)} %param.12) | copy-start | bytes 27652
  42.1 0.8 copy-start.9
  42.1 9.3 %copy-start.12 = (f32[2,2304]{1,0:T(2,128)S(1)}, f32[2,2304]{1,0:T(2,128)}, u32[]{:S(2)}) copy-start(f32[2,2304]{1,0:T(2,128)} %param.11) | copy-start | bytes 55300
  42.1 9.5 %copy-start.13 = (f32[2304]{0:T(1024)S(1)}, f32[2304]{0:T(1024)}, u32[]{:S(2)}) copy-start(f32[2304]{0:T(1024)} %param.13) | copy-start | bytes 27652
  42.1 9.5 %copy-start.14 = (f32[2304]{0:T(1024)S(1)}, f32[2304]{0:T(1024)}, u32[]{:S(2)}) copy-start(f32[2304]{0:T(1024)} %param.14) | copy-start | bytes 27652
  42.1 9.6 %copy-start.7 = (f32[16,2304]{1,0:T(8,128)S(1)}, f32[16,2304]{1,0:T(8,128)}, u32[]{:S(2)}) copy-start(f32[16,2304]{1,0:T(8,128)} %param.15) | copy-start | bytes 442372
  43.6 18.5 %all-to-all-start.1 = ((s32[3,8,576]{2,0,1:T(4,128)}), s32[3,8,576]{2,0,1:T(4,128)}, u32[]{:S(2)}, u32[]{:S(2)}) async-start(s32[3,8,576]{2,0,1:T(4,128)} %broadcast_select_fusion.1), calls=%async_computation.1 | async-start | bytes 163840 | tf_op jit(solution)/shard_map/all_to_all | solution.py:137
  51.8 9.6 %copy-start.10 = (pred[8,576]{1,0:T(8,128)(4,1)S(1)}, pred[8,576]{1,0:T(8,128)(4,1)}, u32[]{:S(2)}) copy-start(pred[8,576]{1,0:T(8,128)(4,1)} %fusion.177) | copy-start | bytes 13828
  61.4 15.5 %copy-start.15 = (s32[144]{0:T(256)S(1)}, s32[144]{0:T(256)}, u32[]{:S(2)}) copy-start(s32[144]{0:T(256)} %iota_add_fusion) | copy-start | bytes 1732
  62.1 13.6 %all-to-all-start = ((f32[8,8,576]{2,0,1:T(8,128)}), f32[8,8,576]{2,0,1:T(8,128)S(1)}, u32[]{:S(2)}, u32[]{:S(2)}) async-start(f32[8,8,576]{2,0,1:T(8,128)} %broadcast_select_fusion), calls=%async_computation | async-start | bytes 327680 | tf_op jit(solution)/shard_map/all_to_all | solution.py:136
  76.9 3.5 %copy-start.6 = (f32[4608,112]{0,1:T(8,128)S(1)}, f32[4608,112]{0,1:T(8,128)}, u32[]{:S(2)}) copy-start(f32[4608,112]{0,1:T(8,128)} %fusion.52) | copy-start | bytes 6193156
  93.0 12.7 %copy-start.4 = (f32[8,4,112,144]{2,3,1,0:T(8,128)}, f32[8,4,112,144]{2,3,1,0:T(8,128)S(1)}, u32[]{:S(2)}) copy-start(f32[8,4,112,144]{2,3,1,0:T(8,128)S(1)} %fusion.91) | copy-start | bytes 6193156
  97.9 5.7 %collective-permute-start = (f32[8,4,8,144]{3,2,1,0:T(8,128)S(1)}, f32[8,4,8,144]{3,2,1,0:T(8,128)S(1)}, u32[]{:S(2)}, u32[]{:S(2)}) collective-permute-start(f32[8,4,8,144]{3,2,1,0:T(8,128)S(1)} %copy.64), channel_id=1, source_target_pairs={{0,4},{4,8},{8,12},{1,5},{5,9},{9,13},{2,6},{6,10},{10,14},{3,7},{... | collective-permute-start | bytes 442376 | tf_op jit(solution)/shard_map/ppermute | solution.py:22
  113.2 8.7 %collective-permute-start.1 = (f32[8,4,8,144]{3,2,1,0:T(8,128)S(1)}, f32[8,4,8,144]{3,2,1,0:T(8,128)S(1)}, u32[]{:S(2)}, u32[]{:S(2)}) collective-permute-start(f32[8,4,8,144]{3,2,1,0:T(8,128)S(1)} %copy.66), channel_id=1, source_target_pairs={{4,0},{8,4},{12,8},{5,1},{9,5},{13,9},{6,2},{10,6},{14,10},{7,3},{... | collective-permute-start | bytes 442376 | tf_op jit(solution)/shard_map/ppermute | solution.py:24
  124.1 3.2 %copy-start.2 = (f32[8,4,8,144]{2,3,1,0:T(8,128)S(1)}, f32[8,4,8,144]{2,3,1,0:T(8,128)}, u32[]{:S(2)}) copy-start(f32[8,4,8,144]{2,3,1,0:T(8,128)} %get-tuple-element.31) | copy-start | bytes 442372
  127.3 1.5 copy-start
  128.8 7.8 %collective-permute-start.2 = (f32[8,4,96,8]{2,3,1,0:T(8,128)}, f32[8,4,96,8]{2,3,1,0:T(8,128)S(1)}, u32[]{:S(2)}, u32[]{:S(2)}) collective-permute-start(f32[8,4,96,8]{2,3,1,0:T(8,128)} %pad_maximum_fusion.8), channel_id=1, source_target_pairs={{0,2},{1,3},{4,6},{5,7},{8,10},{9,11},{12,14},{13,15},{16,18},{17,... | collective-permute-start | bytes 294920 | tf_op jit(solution)/shard_map/ppermute | solution.py:22
  136.6 2.9 %copy-start.1 = (f32[8,4,8,144]{2,3,1,0:T(8,128)S(1)}, f32[8,4,8,144]{2,3,1,0:T(8,128)}, u32[]{:S(2)}) copy-start(f32[8,4,8,144]{2,3,1,0:T(8,128)} %copy-done) | copy-start | bytes 442372
  136.6 2.9 %copy-start.3 = (f32[8,4,8,144]{2,3,1,0:T(8,128)S(1)}, f32[8,4,8,144]{2,3,1,0:T(8,128)}, u32[]{:S(2)}) copy-start(f32[8,4,8,144]{2,3,1,0:T(8,128)} %get-tuple-element.31) | copy-start | bytes 442372
  138.1 7.0 %collective-permute-start.3 = (f32[8,4,96,8]{2,3,1,0:T(8,128)S(1)}, f32[8,4,96,8]{2,3,1,0:T(8,128)S(1)}, u32[]{:S(2)}, u32[]{:S(2)}) collective-permute-start(f32[8,4,96,8]{2,3,1,0:T(8,128)S(1)} %get-tuple-element.30), channel_id=1, source_target_pairs={{2,0},{3,1},{6,4},{7,5},{10,8},{11,9},{14,12},{15,13},{18,16},{19,... | collective-permute-start | bytes 294920 | tf_op jit(solution)/shard_map/ppermute | solution.py:24
  141.0 4.2 %copy-start.5 = (f32[8,4,96,128]{2,3,1,0:T(8,128)S(1)}, f32[8,4,96,128]{2,3,1,0:T(8,128)}, u32[]{:S(2)}) copy-start(f32[8,4,96,128]{2,3,1,0:T(8,128)} %copy.68) | copy-start | bytes 4718596
  145.8 11.6 %collective-permute-start.6 = (f32[4,96,1]{1,2,0:T(1,128)S(1)}, f32[4,96,1]{1,2,0:T(1,128)S(1)}, u32[]{:S(2)}, u32[]{:S(2)}) collective-permute-start(f32[4,96,1]{1,2,0:T(1,128)S(1)} %get-tuple-element.40), channel_id=1, source_target_pairs={{2,0},{3,1},{6,4},{7,5},{10,8},{11,9},{14,12},{15,13},{18,16},{19,... | collective-permute-start | bytes 4616 | tf_op jit(solution)/shard_map/ppermute | solution.py:24
  147.1 16.2 %collective-permute-start.8 = (f32[1,96,128]{1,2,0:T(8,128)S(1)}, f32[1,96,128]{1,2,0:T(8,128)S(1)}, u32[]{:S(2)}, u32[]{:S(2)}) collective-permute-start(f32[1,96,128]{1,2,0:T(8,128)S(1)} %get-tuple-element.36), channel_id=1, source_target_pairs={{1,0},{3,2},{5,4},{7,6},{9,8},{11,10},{13,12},{15,14},{17,16},{19,... | collective-permute-start | bytes 147464 | tf_op jit(solution)/shard_map/ppermute | solution.py:24
  148.4 14.9 %collective-permute-start.9 = (f32[1,96,128]{1,2,0:T(8,128)S(1)}, f32[1,96,128]{1,2,0:T(8,128)S(1)}, u32[]{:S(2)}, u32[]{:S(2)}) collective-permute-start(f32[1,96,128]{1,2,0:T(8,128)S(1)} %get-tuple-element.37), channel_id=1, source_target_pairs={{0,1},{2,3},{4,5},{6,7},{8,9},{10,11},{12,13},{14,15},{16,17},{18,... | collective-permute-start | bytes 147464 | tf_op jit(solution)/shard_map/ppermute | solution.py:22
  151.6 11.7 %collective-permute-start.4 = (f32[4,1,128]{1,2,0:T(8,128)S(1)}, f32[4,1,128]{1,2,0:T(8,128)S(1)}, u32[]{:S(2)}, u32[]{:S(2)}) collective-permute-start(f32[4,1,128]{1,2,0:T(8,128)S(1)} %get-tuple-element.38), channel_id=1, source_target_pairs={{4,0},{8,4},{12,8},{5,1},{9,5},{13,9},{6,2},{10,6},{14,10},{7,3},{... | collective-permute-start | bytes 6152 | tf_op jit(solution)/shard_map/ppermute | solution.py:24
  152.9 10.4 %collective-permute-start.5 = (f32[4,1,128]{1,2,0:T(8,128)S(1)}, f32[4,1,128]{1,2,0:T(8,128)S(1)}, u32[]{:S(2)}, u32[]{:S(2)}) collective-permute-start(f32[4,1,128]{1,2,0:T(8,128)S(1)} %get-tuple-element.39), channel_id=1, source_target_pairs={{0,4},{4,8},{8,12},{1,5},{5,9},{9,13},{2,6},{6,10},{10,14},{3,7},{... | collective-permute-start | bytes 6152 | tf_op jit(solution)/shard_map/ppermute | solution.py:22
  157.4 5.8 %collective-permute-start.7 = (f32[4,96,1]{1,2,0:T(1,128)S(1)}, f32[4,96,1]{1,2,0:T(1,128)S(1)}, u32[]{:S(2)}, u32[]{:S(2)}) collective-permute-start(f32[4,96,1]{1,2,0:T(1,128)S(1)} %get-tuple-element.41), channel_id=1, source_target_pairs={{0,2},{1,3},{4,6},{5,7},{8,10},{9,11},{12,14},{13,15},{16,18},{17,... | collective-permute-start | bytes 4616 | tf_op jit(solution)/shard_map/ppermute | solution.py:22
  164.5 10.9 %all-to-all-start.2 = ((f32[4,128,96]{2,0,1:T(4,128)}), f32[4,128,96]{2,0,1:T(4,128)S(1)}, u32[]{:S(2)}, u32[]{:S(2)}) async-start(f32[4,128,96]{2,0,1:T(4,128)} %copy.69), calls=%async_computation.2 | async-start | bytes 524288 | tf_op jit(solution)/shard_map/all_to_all | solution.py:162
where the time goes:
time: 178 us; the launch traced here: 176 us
  local copies, waits for them, and re-layouts  69.1 us (39%)
  starting transfers between devices  41.3 us (23%)
  other arithmetic  25.5 us (14%)
  waiting for transfers between devices  23.2 us (13%)
  matrix products  16.1 us (9%)
    gather x1, local copies, waits for them, and re-layouts, pack_points(): chosen = order[source_row]  24.1 us
    ppermute x5, starting transfers between devices, padded_2(): lax.ppermute(tail, axis, [(i, (i + 1) % count) for i in range(ends)])  17.3 us
    dot_general x8, matrix products, smear_tile(): lax.dot_general(weighted, weight_y, (((0,), (0,)), ((), ())), preferred_e...  16.1 us
    gather x2, local copies, waits for them, and re-layouts, pack_points(): cell_rows = jnp.where(live[None, :], point_cells[:, chosen], 0)  9.25 us
    ppermute x5, waiting for transfers between devices, padded_2(): lax.ppermute(head, axis, [((i + 1) % count, i) for i in range(ends)])  9.2 us
    gather x2, local copies, waits for them, and re-layouts, pack_points(): force_rows = jnp.where(live[None, :], forces[:, chosen], 0.0)  9.19 us
    slice x3, local copies, waits for them, and re-layouts, spread_rims(): spill_x = jnp.concatenate([padded[:, :, :8], padded[:, :, -8:]], axis=2)  7.66 us
    all_to_all x1, starting transfers between devices, body(): lax.all_to_all(cell_rows, ('gx', 'gy'), split_axis=1, concat_axis=1, tile...  7.25 us
  transfers between devices with their start and end apart: 13, of which 6 were waited for; matrix products, arithmetic and copies ran while one was open for 14% of the time, Pallas kernels for 0%

commit v1 on v0

v1 whole, which is shorter than its diff:
```python
import functools
import math

import jax
import jax.numpy as jnp
from jax import lax
from jax.experimental import pallas as pl
from jax.experimental.pallas import tpu as pltpu
from jax.sharding import PartitionSpec as P

sigma_xy = 3.0
sigma_z = 1.5
reach = 8
tap_total = sum([math.exp(-((float(e) / sigma_xy) ** 2)) for e in range(-8, 9)])
MESH = pl.DeviceIdType.MESH
VM = pl.BlockSpec(memory_space=pltpu.VMEM)
ANY = pl.BlockSpec(memory_space=pl.ANY)
LIMIT = 48 * 1024 * 1024
f32 = jnp.float32
bf16 = jnp.bfloat16


def iota(shape, dim):
    return lax.broadcasted_iota(jnp.int32, shape, dim)


def dot_nt(a, b, precision=None):
    return lax.dot_general(a, b, (((1,), (1,)), ((), ())), precision=precision, preferred_element_type=f32)


def point_forces(inflow, chord_len, twist_base, compliance, blade_frame):
    normal = inflow[0]
    tangent = inflow[1]
    speed_sq = normal * normal + tangent * tangent
    twist_angle = twist_base + compliance * speed_sq
    attack = jnp.arctan2(normal, tangent) - twist_angle
    pressure = 0.5 * speed_sq * chord_len
    lift_force = pressure * (2.0 * math.pi) * jnp.sin(attack)
    drag_force = pressure * (0.01 + 0.5 * attack * attack)
    half = blade_frame.shape[0] // 2
    return blade_frame[:half] * lift_force[None, :] + blade_frame[half:] * drag_force[None, :]


def pack_kernel(tiles, cap, data_ref, owner_ref, out_ref, slot_ref, split_ref, packed_ref):
    points = data_ref.shape[1]
    step = 256
    tri = (iota((step, step), 0) < iota((step, step), 1)).astype(f32).astype(bf16)
    carry = jnp.zeros((tiles, 1), f32)
    for k in range(points // step):
        here = owner_ref[:, k * step : (k + 1) * step]
        hot = (iota((tiles, step), 0) == here).astype(f32)
        rank = jnp.dot(hot.astype(bf16), tri, preferred_element_type=f32)
        position = jnp.sum(hot * (rank + carry), axis=0, keepdims=True)
        carry = carry + jnp.sum(hot, axis=1, keepdims=True)
        slot_ref[:, k * step : (k + 1) * step] = position.astype(jnp.int32) + here * cap
    data = data_ref[...]
    high = data.astype(bf16)
    split_ref[0:16, :] = high
    split_ref[16:32, :] = (data - high.astype(f32)).astype(bf16)
    block = 512
    slots = packed_ref.shape[1]

    def one(j, unused):
        first = pl.multiple_of(j * block, block)
        total = jnp.zeros((32, block), f32)
        part = 768
        for k in range(points // part):
            goal = slot_ref[:, k * part : (k + 1) * part] - first
            hot = jnp.where(iota((block, part), 0) == goal, 1.0, 0.0).astype(bf16)
            total = total + dot_nt(split_ref[:, k * part : (k + 1) * part], hot)
        packed_ref[:, pl.ds(first, block)] = total[0:16] + total[16:32]
        return unused

    lax.fori_loop(0, slots // block, one, 0)
    for t in range(tiles):
        out_ref[t] = packed_ref[:, t * cap : (t + 1) * cap]


def tap_weight(offset):
    scaled = offset.astype(f32) * (1.0 / sigma_xy)
    return jnp.where(jnp.abs(offset) <= reach, jnp.exp(-scaled * scaled) * (1.0 / tap_total), 0.0)


def smear_kernel(
    sources, cap, channels, levels, levels_all, wx, wy, in_ref, center_ref, xs_ref, ys_ref, cn_ref, rows_ref, a_ref, b_ref, h_ref, acc_ref, hacc_ref
):
    px = wx + 16
    slots = sources * cap
    rows_ref[...] = jnp.zeros(rows_ref.shape, f32)
    for s in range(sources):
        rows_ref[:, s * cap : (s + 1) * cap] = in_ref[s]
    first_level = lax.axis_index("gz") * levels
    acc_ref[...] = jnp.zeros(acc_ref.shape, f32)
    hacc_ref[...] = jnp.zeros(hacc_ref.shape, f32)
    chunk = a_ref.shape[1]

    def one(j, unused):
        lanes = pl.ds(pl.multiple_of(j * chunk, chunk), chunk)
        cells = rows_ref[8:16, lanes].astype(jnp.int32)
        x, y, z = cells[0:1], cells[1:2], cells[2:3]
        gx = tap_weight(iota((px, chunk), 0) - reach - x)
        for c in range(channels):
            a_ref[c * px : (c + 1) * px, :] = (rows_ref[c : c + 1, lanes] * gx).astype(bf16)
        every = (iota((levels_all, chunk), 0) - z).astype(f32) * (1.0 / sigma_z)
        total = 1.0 / jnp.sum(jnp.exp(-every * every), axis=0, keepdims=True)
        gy = tap_weight(iota((wy + 16, chunk), 0) - reach - y).astype(bf16).astype(f32)
        for k in range(levels):
            near = (first_level + k - z).astype(f32) * (1.0 / sigma_z)
            gz = jnp.exp(-near * near) * total
            b_ref[k * wy : (k + 1) * wy, :] = (gy[8 : 8 + wy] * gz).astype(bf16)
            rims = jnp.concatenate([gy[0:8] * gz, gy[8 + wy :] * gz], axis=0)
            h_ref[k * 16 : (k + 1) * 16, :] = rims.astype(bf16)
        acc_ref[...] += dot_nt(a_ref[...], b_ref[...])
        hacc_ref[...] += dot_nt(h_ref[...], a_ref[...])
        return unused

    lax.fori_loop(0, rows_ref.shape[1] // chunk, one, 0)
    for c in range(channels):
        center_ref[c] = acc_ref[c * px + 8 : c * px + 8 + wx, :]
        xs_ref[0, c] = acc_ref[c * px : c * px + 8, :]
        xs_ref[1, c] = acc_ref[c * px + 8 + wx : (c + 1) * px, :]
        for k in range(levels):
            for side in range(2):
                rim = hacc_ref[k * 16 + side * 8 : k * 16 + side * 8 + 8, c * px : (c + 1) * px]
                ys_ref[side, c, k * 8 : (k + 1) * 8, :] = rim[:, 8 : 8 + wx]
                cn_ref[side, 0, k * 8 : (k + 1) * 8, c * 8 : (c + 1) * 8] = rim[:, 0:8]
                cn_ref[side, 1, k * 8 : (k + 1) * 8, c * 8 : (c + 1) * 8] = rim[:, 8 + wx :]


def place():
    return (lax.axis_index("group"), lax.axis_index("gx"), lax.axis_index("gy"), lax.axis_index("gz"))


def rim_kernel(nx, ny, xs_ref, ys_ref, cn_ref, rx_ref, ry_ref, rc_ref, send_sem, recv_sem):
    g, x, y, z = place()
    barrier = pltpu.get_barrier_semaphore()
    moves = [(dx, dy) for dx in (-1, 0, 1) for dy in (-1, 0, 1) if (dx, dy) != (0, 0)]

    def there(dx, dy):
        return (x + dx >= 0) & (x + dx < nx) & (y + dy >= 0) & (y + dy < ny)

    def copy(i, dx, dy):
        high_x, high_y = (dx + 1) // 2, (dy + 1) // 2
        if dy == 0:
            src, dst = xs_ref.at[high_x], rx_ref.at[1 - high_x]
        elif dx == 0:
            src, dst = ys_ref.at[high_y], ry_ref.at[1 - high_y]
        else:
            src, dst = cn_ref.at[high_y, high_x], rc_ref.at[1 - high_y, 1 - high_x]
        return pltpu.make_async_remote_copy(
            src_ref=src, dst_ref=dst, send_sem=send_sem.at[i], recv_sem=recv_sem.at[i],
            device_id=(g, x + dx, y + dy, z), device_id_type=MESH,
        )

    count = jnp.int32(0)
    for dx, dy in moves:
        count = count + there(dx, dy).astype(jnp.int32)

        @pl.when(there(dx, dy))
        def _():
            pl.semaphore_signal(barrier, inc=1, device_id=(g, x + dx, y + dy, z), device_id_type=MESH)

    pl.semaphore_wait(barrier, count)
    for i, (dx, dy) in enumerate(moves):

        @pl.when(there(dx, dy))
        def _():
            copy(i, dx, dy).start()

    for i, (dx, dy) in enumerate(moves):

        @pl.when(there(dx, dy))
        def _():
            copy(i, dx, dy).wait_send()

        @pl.when(there(-dx, -dy))
        def _():
            copy(i, dx, dy).wait_recv()


def state_kernel(nx, ny, base_ref, tend_ref, center_ref, rx_ref, ry_ref, rc_ref, out_ref):
    unused_g, x, y, unused_z = place()
    c = pl.program_id(0)
    levels, wx, wy = base_ref.shape[1:]
    low_x, high_x, low_y, high_y = x > 0, x < nx - 1, y > 0, y < ny - 1
    strips = []
    for side, ok_y in ((0, low_y), (1, high_y)):
        strip = jnp.where(ok_y, ry_ref[side, 0], 0.0)
        for end, ok_x in ((0, low_x), (1, high_x)):
            corner = jnp.where(ok_y & ok_x, rc_ref[side, end], 0.0)
            size = corner.shape[1]
            row, col = iota((size, wx), 0), iota((size, wx), 1)
            put = ((row - c * 8 == col - end * (wx - 8)) & (row >= c * 8) & (row < c * 8 + 8)).astype(f32)
            strip = strip + jnp.dot(corner, put, precision=lax.Precision.HIGHEST, preferred_element_type=f32)
        strips.append(strip)
    strip = jnp.concatenate(strips, axis=0)
    half = levels * 8
    row, col = iota((2 * half, levels * wy), 0), iota((2 * half, levels * wy), 1)
    side, level, cell = row // half, (row % half) // 8, row % 8
    put = (col == level * wy + cell + side * (wy - 8)).astype(f32)
    source = center_ref[0] + lax.dot_general(
        strip, put, (((0,), (0,)), ((), ())), precision=lax.Precision.HIGHEST, preferred_element_type=f32
    )
    source = jnp.concatenate(
        [
            source[:8] + jnp.where(low_x, rx_ref[0, 0], 0.0),
            source[8:-8],
            source[-8:] + jnp.where(high_x, rx_ref[1, 0], 0.0),
        ],
        axis=0,
    )
    for k in range(levels):
        out_ref[0, k] = base_ref[0, k] + 0.5 * (tend_ref[0, k].astype(f32) + source[:, k * wy : (k + 1) * wy])


def lines_kernel(nx, ny, nz, fs_ref, out_ref, su, sv, ru, rv, rw, lines, land, hs, hr, ls, lr):
    g, x, y, z = place()
    unused, levels, wx, wy = fs_ref.shape
    barrier = pltpu.get_barrier_semaphore()

    def at(axis, d):
        return (g, x + d if axis == 0 else x, y + d if axis == 1 else y, z + d if axis == 2 else z)

    def there(axis, d):
        here, count = ((x, nx), (y, ny), (z, nz))[axis]
        return (here + d >= 0) & (here + d < count)

    for k in range(1, nx):
        pl.semaphore_signal(barrier, inc=1, device_id=(g, lax.rem(x + k, nx), y, z), device_id_type=MESH)
    count = jnp.int32(nx - 1)
    for axis in (1, 2):
        for d in (-1, 1):
            count = count + there(axis, d).astype(jnp.int32)

            @pl.when(there(axis, d))
            def _():
                pl.semaphore_signal(barrier, inc=1, device_id=at(axis, d), device_id_type=MESH)

    across = [jnp.transpose(fs_ref[1, k]) for k in range(levels)]
    for k in range(levels):
        su[0, k : k + 1, :] = fs_ref[0, k, 0:1, :]
        su[1, k : k + 1, :] = fs_ref[0, k, wx - 1 : wx, :]
        sv[0, k : k + 1, :] = across[k][0:1]
        sv[1, k : k + 1, :] = across[k][wy - 1 : wy]
    pl.semaphore_wait(barrier, count)

    def halo(axis, d):
        i = axis * 2 + (d + 1) // 2
        high = (d + 1) // 2
        if axis == 0:
            src, dst = su.at[high], ru.at[1 - high]
        elif axis == 1:
            src, dst = sv.at[high], rv.at[1 - high]
        else:
            src, dst = fs_ref.at[2, (levels - 1) * high], rw.at[1 - high]
        return pltpu.make_async_remote_copy(
            src_ref=src, dst_ref=dst, send_sem=hs.at[i], recv_sem=hr.at[i], device_id=at(axis, d), device_id_type=MESH
        )

    moves = [(axis, d) for axis in range(3) for d in (-1, 1)]
    for axis, d in moves:

        @pl.when(there(axis, d))
        def _():
            halo(axis, d).start()

        @pl.when(jnp.logical_not(there(axis, d)))
        def _():
            into = (ru, rv, rw)[axis]
            into[(d + 1) // 2] = jnp.zeros(into.shape[1:], f32)

    for axis, d in moves:

        @pl.when(there(axis, d))
        def _():
            halo(axis, d).wait_send()

        @pl.when(there(axis, -d))
        def _():
            halo(axis, d).wait_recv()

    band = wy // nx
    for k in range(levels):
        u = fs_ref[0, k]
        along = jnp.concatenate([u[1:], ru[1, k : k + 1, :]], axis=0) - jnp.concatenate([ru[0, k : k + 1, :], u[:-1]], axis=0)
        above = fs_ref[2, k + 1] if k + 1 < levels else rw[1]
        below = fs_ref[2, k - 1] if k > 0 else rw[0]
        v = across[k]
        over = jnp.concatenate([v[1:], rv[1, k : k + 1, :]], axis=0) - jnp.concatenate([rv[0, k : k + 1, :], v[:-1]], axis=0)
        div = 0.5 * (jnp.transpose(along + (above - below)) + over)
        for j in range(nx):
            lines[j, k] = div[j * band : (j + 1) * band]

    def line(k):
        far = lax.rem(x + k, nx)
        return pltpu.make_async_remote_copy(
            src_ref=lines.at[far], dst_ref=land.at[x], send_sem=ls.at[k], recv_sem=lr.at[k],
            device_id=(g, far, y, z), device_id_type=MESH,
        )

    def arrival(k):
        far = lax.rem(x + nx - k, nx)
        return pltpu.make_async_remote_copy(
            src_ref=lines.at[far], dst_ref=land.at[far], send_sem=ls.at[k], recv_sem=lr.at[k],
            device_id=(g, far, y, z), device_id_type=MESH,
        )

    for k in range(1, nx):
        line(k).start()
    land[x] = lines[x]
    for k in range(1, nx):
        line(k).wait_send()
        arrival(k).wait_recv()
    for j in range(nx):
        out_ref[:, :, j * wx : (j + 1) * wx] = land[j]


def params(collective_id=None):
    if collective_id is None:
        return pltpu.CompilerParams(vmem_limit_bytes=LIMIT)
    return pltpu.CompilerParams(vmem_limit_bytes=LIMIT, collective_id=collective_id, has_side_effects=True)


def body(base_state, tendency, inflow, chord_len, twist_base, compliance, blade_frame, owner_tile, point_cells):
    nx, ny, nz = lax.axis_size("gx"), lax.axis_size("gy"), lax.axis_size("gz")
    tiles = nx * ny
    points = owner_tile.shape[0]
    cap = max(2, (2 * points + tiles - 1) // tiles)
    channels, levels, wx, wy = base_state.shape
    px = wx + 16
    forces = point_forces(inflow, chord_len, twist_base, compliance, blade_frame)
    data = jnp.concatenate([forces, point_cells.astype(f32), jnp.zeros((5, points), f32)], axis=0)
    slots = -(-tiles * cap // 512) * 512
    shape = jax.ShapeDtypeStruct
    packed = pl.pallas_call(
        functools.partial(pack_kernel, tiles, cap),
        out_shape=shape((tiles, 16, cap), f32),
        in_specs=[VM, VM],
        out_specs=VM,
        scratch_shapes=[pltpu.VMEM((1, points), jnp.int32), pltpu.VMEM((32, points), bf16), pltpu.VMEM((16, slots), f32)],
        compiler_params=params(),
        name="pack_points",
    )(data, owner_tile.reshape(1, points))
    arrived = lax.all_to_all(packed, ("gx", "gy"), split_axis=0, concat_axis=0, tiled=True)
    chunk = 512
    center, xs, ys, cn = pl.pallas_call(
        functools.partial(smear_kernel, tiles, cap, channels, levels, levels * nz, wx, wy),
        out_shape=(
            shape((channels, wx, levels * wy), f32),
            shape((2, channels, 8, levels * wy), f32),
            shape((2, channels, levels * 8, wx), f32),
            shape((2, 2, levels * 8, channels * 8), f32),
        ),
        in_specs=[VM],
        out_specs=(VM,) * 4,
        scratch_shapes=[
            pltpu.VMEM((16, slots), f32),
            pltpu.VMEM((channels * px, chunk), bf16),
            pltpu.VMEM((levels * wy, chunk), bf16),
            pltpu.VMEM((levels * 16, chunk), bf16),
            pltpu.VMEM((channels * px, levels * wy), f32),
            pltpu.VMEM((levels * 16, channels * px), f32),
        ],
        compiler_params=params(),
        name="smear_points",
    )(arrived)
    rx, ry, rc = pl.pallas_call(
        functools.partial(rim_kernel, nx, ny),
        out_shape=(shape(xs.shape, f32), shape(ys.shape, f32), shape(cn.shape, f32)),
        in_specs=[ANY] * 3,
        out_specs=(ANY,) * 3,
        scratch_shapes=[pltpu.SemaphoreType.DMA((8,)), pltpu.SemaphoreType.DMA((8,))],
        compiler_params=params(1),
        name="exchange_rims",
    )(xs, ys, cn)
    forced_state = pl.pallas_call(
        functools.partial(state_kernel, nx, ny),
        grid=(channels,),
        out_shape=shape(base_state.shape, f32),
        in_specs=[
            pl.BlockSpec((1, levels, wx, wy), lambda c: (c, 0, 0, 0)),
            pl.BlockSpec((1, levels, wx, wy), lambda c: (c, 0, 0, 0)),
            pl.BlockSpec((1, wx, levels * wy), lambda c: (c, 0, 0)),
            pl.BlockSpec((2, 1, 8, levels * wy), lambda c: (0, c, 0, 0)),
            pl.BlockSpec((2, 1, levels * 8, wx), lambda c: (0, c, 0, 0)),
            pl.BlockSpec(cn.shape, lambda c: (0, 0, 0, 0)),
        ],
        out_specs=pl.BlockSpec((1, levels, wx, wy), lambda c: (c, 0, 0, 0)),
        compiler_params=params(),
        name="forced_state",
    )(base_state, tendency, center, rx, ry, rc)
    band = wy // nx
    divergence_lines = pl.pallas_call(
        functools.partial(lines_kernel, nx, ny, nz),
        grid=(1,),
        out_shape=shape((levels, band, nx * wx), f32),
        in_specs=[pl.BlockSpec((3, levels, wx, wy), lambda i: (0, 0, 0, 0))],
        out_specs=pl.BlockSpec((levels, band, nx * wx), lambda i: (0, 0, 0)),
        scratch_shapes=[
            pltpu.VMEM((2, levels, wy), f32),
            pltpu.VMEM((2, levels, wx), f32),
            pltpu.VMEM((2, levels, wy), f32),
            pltpu.VMEM((2, levels, wx), f32),
            pltpu.VMEM((2, wx, wy), f32),
            pltpu.VMEM((nx, levels, band, wx), f32),
            pltpu.VMEM((nx, levels, band, wx), f32),
            pltpu.SemaphoreType.DMA((6,)),
            pltpu.SemaphoreType.DMA((6,)),
            pltpu.SemaphoreType.DMA((nx,)),
            pltpu.SemaphoreType.DMA((nx,)),
        ],
        compiler_params=params(2),
        name="divergence_lines",
    )(forced_state)
    return (forced_state, divergence_lines)


def solution(mesh):
    in_specs = (
        P("group", "gz", "gx", "gy"),
        P("group", "gz", "gx", "gy"),
        P("group", ("gx", "gy")),
        P(("group", "gx", "gy")),
        P(("group", "gx", "gy")),
        P(("group", "gx", "gy")),
        P("group", ("gx", "gy")),
        P(("gx", "gy"), "group"),
        P("group", ("gx", "gy")),
    )
    out_specs = (P("group", "gz", "gx", "gy"), P(("group", "gz"), ("gy", "gx"), None))
    return jax.shard_map(body, mesh=mesh, in_specs=in_specs, out_specs=out_specs, check_vma=False)
```

time: 178 us -> 65.3 us (0.37)
  local copies, waits for them, and re-layouts: 69.1 us -> 2.87 us
  starting transfers between devices: 41.3 us -> 0 us
  Pallas kernels: 0 us -> 38.9 us
  waiting for transfers between devices: 23.2 us -> 0 us
  other arithmetic: 25.5 us -> 4.38 us
  blocking collectives: 0 us -> 18 us
  matrix products: 16.1 us -> 0 us
    gather x5 -> x0, local copies, waits for them, and re-layouts: 42.5 us -> none  [the longest x1 24.1 us: pack_points(): chosen = order[source_row]]
    pallas_call x0 -> x5, Pallas kernels: none -> 38.9 us  [the longest x1 10.5 us: body(): pl.pallas_call(functools.partial(lines_kernel, nx, ny, nz), grid=(1,), ou...]
    ppermute x10 -> x0, starting transfers between devices: 23.9 us -> none  [the longest x5 17.3 us: padded_2(): lax.ppermute(tail, axis, [(i, (i + 1) % count) for i in range(ends)])]
    all_to_all x0 -> x1, blocking collectives: none -> 18 us  [body(): lax.all_to_all(packed, ('gx', 'gy'), split_axis=0, concat_axis=0, tiled=T...]
    all_to_all x3 -> x0, starting transfers between devices: 17.4 us -> none  [the longest x1 7.25 us: body(): lax.all_to_all(cell_rows, ('gx', 'gy'), split_axis=1, concat_axis=1, tile...]
    dot_general x8 -> x0, matrix products: 16.1 us -> none  [smear_tile(): lax.dot_general(weighted, weight_y, (((0,), (0,)), ((), ())), preferred_e...]
    ppermute x10 -> x0, waiting for transfers between devices: 14.4 us -> none  [the longest x5 9.2 us: padded_2(): lax.ppermute(head, axis, [((i + 1) % count, i) for i in range(ends)])]
    slice x10 -> x0, local copies, waits for them, and re-layouts: 11.9 us -> none  [the longest x3 7.66 us: spread_rims(): spill_x = jnp.concatenate([padded[:, :, :8], padded[:, :, -8:]], axis=2)]
  transfers between devices with their start and end apart: 13 -> 0, of which waited for: 6 -> 0; matrix products, arithmetic and copies ran while one was open for 14% -> 0% of each run, Pallas kernels for 0% -> 0%
where the time goes in v1:
time: 65.3 us; the launch traced here: 64.8 us
  Pallas kernels  38.9 us (60%)
  blocking collectives  18 us (28%)
  other arithmetic  4.38 us (7%)
  local copies, waits for them, and re-layouts  2.87 us (4%)
  between operations  0.72 us (1%)
    all_to_all x1, blocking collectives, body(): lax.all_to_all(packed, ('gx', 'gy'), split_axis=0, concat_axis=0, tiled=T...  18 us
    pallas_call x1, Pallas kernels, body(): pl.pallas_call(functools.partial(lines_kernel, nx, ny, nz), grid=(1,), ou...  10.5 us
    pallas_call x1, Pallas kernels, body(): pl.pallas_call(functools.partial(smear_kernel, tiles, cap, channels, leve...  9.62 us
    pallas_call x1, Pallas kernels, body(): pl.pallas_call(functools.partial(pack_kernel, tiles, cap), out_shape=shap...  7.49 us
    pallas_call x1, Pallas kernels, body(): pl.pallas_call(functools.partial(state_kernel, nx, ny), grid=(channels,),...  5.79 us
    pallas_call x1, Pallas kernels, body(): pl.pallas_call(functools.partial(rim_kernel, nx, ny), out_shape=(shape(xs...  5.55 us
    unnamed x9, local copies, waits for them, and re-layouts  2.79 us

profile of v1, /device:TPU:0, one launch (start us, length us, event | category | flops | bytes accessed | tf_op | source)
XLA Modules:
  0.0 64.8 jit_solution(4889135834359556061)
XLA Ops:
  0.6 0.0 copy-start.2
  0.6 0.0 copy-start.1
  0.6 1.1 %add_reduce_fusion = (f32[2304]{0:T(1024)S(1)}, f32[2304]{0:T(1024)S(1)}) fusion(f32[2,2304]{1,0:T(2,128)} %param.11), kind=kLoop, calls=%fused_computation.9 | loop fusion | flops 6912 | bytes 36864 | tf_op jit(solution)/shard_map/add | solution.py:34
  1.7 0.8 %sine_multiply_fusion = (f32[2304]{0:T(1024)S(1)}, f32[2304]{0:T(1024)S(1)}) fusion(f32[2304]{0:T(1024)} %param.12, f32[2304]{0:T(1024)S(1)} %get-tuple-element.16, f32[2304]{0:T(1024)S(1)} %get-tuple-element.17, f32[2304]{0:T(1024)} %param.13, f32[2304]{0:T(1024)} %param.14), kind=kLoop, calls=%fused_computation.5 | loop fusion | flops 16128 | bytes 64512 | tf_op jit(solution)/shard_map/mul | solution.py:38
  2.5 0.7 %fusion.1 = f32[2304]{0:T(1024)S(1)} fusion(f32[2304]{0:T(1024)S(1)} %get-tuple-element.19, f32[2304]{0:T(1024)} %param.12, f32[2304]{0:T(1024)S(1)} %get-tuple-element.16), kind=kLoop, calls=%fused_computation.4 | loop fusion | flops 13824 | bytes 36864 | tf_op jit(solution)/shard_map/mul | solution.py:39
  3.2 0.8 %convert_element_type.3 = f32[3,2304]{1,0:T(4,128)S(1)} convert(s32[3,2304]{1,0:T(4,128)} %param.17) | non-fusion elementwise | flops 6912 | bytes 55296 | tf_op jit(solution)/shard_map/convert_element_type | solution.py:332
  4.0 0.1 pad.2.clone
  4.1 0.9 %multiply_add_fusion = f32[8,2304]{1,0:T(8,128)S(1)} fusion(f32[16,2304]{1,0:T(8,128)} %param.15, f32[2304]{0:T(1024)S(1)} %fusion.1, f32[2304]{0:T(1024)S(1)} %get-tuple-element.18), kind=kLoop, calls=%fused_computation.1 | loop fusion | flops 55296 | bytes 239616 | tf_op jit(solution)/shard_map/add | solution.py:41
  5.0 0.1 maximum_maximum_fusion.data_ref
  5.1 0.0 copy-start.3
  5.1 0.7 %copy-done.3 = s32[2304,1]{0,1:T(1,128)S(1)} copy-done((s32[2304,1]{0,1:T(1,128)S(1)}, s32[2304,1]{0,1:T(1,128)}, u32[]{:S(2)}) %copy-start.3) | copy-done | bytes 9240
  5.8 7.5 %pack_points.1 = f32[8,16,576]{2,1,0:T(8,128)S(1)} custom-call(f32[16,2304]{1,0:T(8,128)S(1)} %maximum_maximum_fusion.data_ref, s32[1,2304]{1,0:T(1,128)S(1)} %bitcast.1), custom_call_target="tpu_custom_call" | custom-call | tf_op jit(solution)/shard_map/pack_points/pallas_call | solution.py:335
  13.3 18.0 %all_to_all.5.in_ref = f32[8,16,576]{2,1,0:T(8,128)S(1)} all-to-all(f32[8,16,576]{2,1,0:T(8,128)S(1)} %pack_points.1), channel_id=1, replica_groups=mesh['group'=2,'gx'=4,'gy'=2,'gz'=2] {'gx','gy'}, dimensions={0} | all-to-all | bytes 589824 | tf_op jit(solution)/shard_map/all_to_all | solution.py:344
  31.3 9.6 %smear_points.1 = (f32[8,96,512]{2,1,0:T(8,128)S(1)}, f32[2,8,8,512]{3,2,1,0:T(8,128)S(1)}, f32[2,8,32,96]{3,2,1,0:T(8,128)S(1)}, f32[2,2,32,64]{3,2,1,0:T(8,128)S(1)}) custom-call(f32[8,16,576]{2,1,0:T(8,128)S(1)} %all_to_all.5.in_ref), custom_call_target="tpu_custom_call" | custom-call | tf_op jit(solution)/shard_map/smear_points/pallas_call | solution.py:346
  40.9 5.5 %exchange_rims.1 = (f32[2,8,8,512]{3,2,1,0:T(8,128)S(1)}, f32[2,8,32,96]{3,2,1,0:T(8,128)S(1)}, f32[2,2,32,64]{3,2,1,0:T(8,128)S(1)}) custom-call(f32[2,8,8,512]{3,2,1,0:T(8,128)S(1)} %get-tuple-element.10.xs_ref, f32[2,8,32,96]{3,2,1,0:T(8,128)S(1)} %get-tuple-element.11.ys_ref, f32[2,2,32,64]{3,2,1,0:T(8,128)S(1)} %get-tuple-element.12.cn_ref), custom_call_target="tpu_custom_call" | custom-call | tf_op jit(solution)/shard_map/exchange_rims/pallas_call | solution.py:367
  46.5 0.0 copy-done.2
  46.5 0.0 copy-done.1
  46.5 5.8 %forced_state.1.fs_ref = f32[8,4,96,128]{3,2,1,0:T(8,128)} custom-call(f32[8,4,96,128]{3,2,1,0:T(8,128)S(1)} %copy-done.1, bf16[8,4,96,128]{3,2,1,0:T(8,128)(2,1)S(1)} %copy-done.2, f32[8,96,512]{2,1,0:T(8,128)S(1)} %get-tuple-element.9.center_ref, f32[2,8,8,512]{3,2,1,0:T(8,128)S(1)} %get-tuple-element.13.rx_ref, ...), custom_call_target="tpu_custom_call" | custom-call | tf_op jit(solution)/shard_map/forced_state/pallas_call | solution.py:376
  52.3 0.0 copy-start
  52.3 1.4 %copy-done = f32[8,4,96,128]{3,2,1,0:T(8,128)S(1)} copy-done((f32[8,4,96,128]{3,2,1,0:T(8,128)S(1)}, f32[8,4,96,128]{3,2,1,0:T(8,128)}, u32[]{:S(2)}) %copy-start) | copy-done | bytes 1572888
  53.7 10.5 %divergence_lines.1 = f32[4,32,384]{2,1,0:T(8,128)S(1)} custom-call(f32[8,4,96,128]{3,2,1,0:T(8,128)S(1)} %copy-done), custom_call_target="tpu_custom_call" | custom-call | tf_op jit(solution)/shard_map/divergence_lines/pallas_call | solution.py:393
  64.2 0.7 %copy.12 = f32[4,32,384]{2,1,0:T(8,128)} copy(f32[4,32,384]{2,1,0:T(8,128)S(1)} %divergence_lines.1) | data formatting | bytes 393216
  (1 shorter events, 0.0 us)
Async XLA Ops:
  0.6 45.8 %copy-start.2 = (bf16[8,4,96,128]{3,2,1,0:T(8,128)(2,1)S(1)}, bf16[8,4,96,128]{3,2,1,0:T(8,128)(2,1)}, u32[]{:S(2)}) copy-start(bf16[8,4,96,128]{3,2,1,0:T(8,128)(2,1)} %tend_ref.1) | copy-start | bytes 2359300
  0.6 45.8 %copy-start.1 = (f32[8,4,96,128]{3,2,1,0:T(8,128)S(1)}, f32[8,4,96,128]{3,2,1,0:T(8,128)}, u32[]{:S(2)}) copy-start(f32[8,4,96,128]{3,2,1,0:T(8,128)} %base_ref.1) | copy-start | bytes 4718596
  5.1 0.7 %copy-start.3 = (s32[2304,1]{0,1:T(1,128)S(1)}, s32[2304,1]{0,1:T(1,128)}, u32[]{:S(2)}) copy-start(s32[2304,1]{0,1:T(1,128)} %param.16) | copy-start | bytes 27652
  52.3 1.4 %copy-start = (f32[8,4,96,128]{3,2,1,0:T(8,128)S(1)}, f32[8,4,96,128]{3,2,1,0:T(8,128)}, u32[]{:S(2)}) copy-start(f32[8,4,96,128]{3,2,1,0:T(8,128)} %forced_state.1.fs_ref) | copy-start | bytes 4718596

commit v2 on v1

--- a/solution.py
+++ b/solution.py
@@ -28,35 +28,44 @@
     return lax.dot_general(a, b, (((1,), (1,)), ((), ())), precision=precision, preferred_element_type=f32)
 
 
-def point_forces(inflow, chord_len, twist_base, compliance, blade_frame):
-    normal = inflow[0]
-    tangent = inflow[1]
-    speed_sq = normal * normal + tangent * tangent
-    twist_angle = twist_base + compliance * speed_sq
-    attack = jnp.arctan2(normal, tangent) - twist_angle
-    pressure = 0.5 * speed_sq * chord_len
-    lift_force = pressure * (2.0 * math.pi) * jnp.sin(attack)
-    drag_force = pressure * (0.01 + 0.5 * attack * attack)
-    half = blade_frame.shape[0] // 2
-    return blade_frame[:half] * lift_force[None, :] + blade_frame[half:] * drag_force[None, :]
-
-
-def pack_kernel(tiles, cap, data_ref, owner_ref, out_ref, slot_ref, split_ref, packed_ref):
-    points = data_ref.shape[1]
+def arc_tangent(n, t):
+    small, large = jnp.minimum(n, t), jnp.maximum(n, t)
+    upper = small > 0.41421356 * large
+    r = jnp.where(upper, small - large, small) / jnp.where(upper, small + large, large)
+    q = r * r
+    poly = ((8.05374449538e-2 * q - 1.38776856032e-1) * q + 1.99777106478e-1) * q - 3.33329491539e-1
+    angle = jnp.where(upper, math.pi / 4, 0.0) + (poly * q * r + r)
+    return jnp.where(n > t, math.pi / 2 - angle, angle)
+
+
+def pack_kernel(
+    tiles, cap, half, inflow_ref, chord_ref, twist_ref, compliance_ref, frame_ref, owner_ref, cells_ref, out_ref, slot_ref, split_ref, packed_ref
+):
+    points = owner_ref.shape[1]
     step = 256
     tri = (iota((step, step), 0) < iota((step, step), 1)).astype(f32).astype(bf16)
     carry = jnp.zeros((tiles, 1), f32)
+    mine = lax.axis_index("gz") * half
+    wide = -(-cap // 128) * 128
     for k in range(points // step):
         here = owner_ref[:, k * step : (k + 1) * step]
         hot = (iota((tiles, step), 0) == here).astype(f32)
         rank = jnp.dot(hot.astype(bf16), tri, preferred_element_type=f32)
         position = jnp.sum(hot * (rank + carry), axis=0, keepdims=True)
         carry = carry + jnp.sum(hot, axis=1, keepdims=True)
-        slot_ref[:, k * step : (k + 1) * step] = position.astype(jnp.int32) + here * cap
-    data = data_ref[...]
-    high = data.astype(bf16)
-    split_ref[0:16, :] = high
-    split_ref[16:32, :] = (data - high.astype(f32)).astype(bf16)
+        slot_ref[:, k * step : (k + 1) * step] = position.astype(jnp.int32) + (here - mine) * wide
+    normal, tangent = inflow_ref[0:1, :], inflow_ref[1:2, :]
+    speed_sq = normal * normal + tangent * tangent
+    attack = arc_tangent(normal, tangent) - (twist_ref[...] + compliance_ref[...] * speed_sq)
+    pressure = 0.5 * speed_sq * chord_ref[...]
+    lift = pressure * (2.0 * math.pi) * jnp.sin(attack)
+    drag = pressure * (0.01 + 0.5 * attack * attack)
+    channels = frame_ref.shape[0] // 2
+    forces = frame_ref[:channels, :] * lift + frame_ref[channels:, :] * drag
+    high = forces.astype(bf16).astype(f32)
+    cells = jnp.concatenate([cells_ref[...].astype(f32), jnp.zeros((13, points), f32)], axis=0)
+    split_ref[0:16, :] = jnp.concatenate([high, forces - high], axis=0).astype(bf16)
+    split_ref[16:32, :] = cells.astype(bf16)
     block = 512
     slots = packed_ref.shape[1]
 
@@ -68,12 +77,122 @@
             goal = slot_ref[:, k * part : (k + 1) * part] - first
             hot = jnp.where(iota((block, part), 0) == goal, 1.0, 0.0).astype(bf16)
             total = total + dot_nt(split_ref[:, k * part : (k + 1) * part], hot)
-        packed_ref[:, pl.ds(first, block)] = total[0:16] + total[16:32]
+        packed_ref[0:8, pl.ds(first, block)] = total[0:8] + total[8:16]
+        packed_ref[8:16, pl.ds(first, block)] = total[16:24]
         return unused
 
     lax.fori_loop(0, slots // block, one, 0)
-    for t in range(tiles):
-        out_ref[t] = packed_ref[:, t * cap : (t + 1) * cap]
+    pieces = wide // 128
+    for t in range(half):
+        out_ref[t] = jnp.zeros(out_ref.shape[1:], f32)
+        out_ref[t, :, 0:wide] = packed_ref[0:8, t * wide : (t + 1) * wide]
+        for i in range(3):
+            for j in range(pieces):
+                row = i * pieces + j
+                out_ref[t, row % 8 : row % 8 + 1, wide + row // 8 * 128 : wide + row // 8 * 128 + 128] = packed_ref[
+                    8 + i : 9 + i, t * wide + j * 128 : t * wide + (j + 1) * 128
+                ]
+
+
+def points_kernel(tiles, cap, half, ny, in_ref, out_ref, land, send_sem, recv_sem, out_sem, pass_sem):
+    g, x, y, z = place()
+    me = x * ny + y
+    owns = me // half == z
+    barrier = pltpu.get_barrier_semaphore()
+
+    def device(t):
+        return (g, t // ny, t % ny, z)
+
+    sibling = (g, x, y, 1 - z)
+
+    @pl.when(owns)
+    def _():
+        def greet(k, unused):
+            pl.semaphore_signal(barrier, inc=1, device_id=device(lax.rem(me + k, tiles)), device_id_type=MESH)
+            return unused
+
+        lax.fori_loop(1, tiles, greet, 0)
+
+    pl.semaphore_signal(barrier, inc=1, device_id=sibling, device_id_type=MESH)
+    pl.semaphore_wait(barrier, half + 1 - owns.astype(jnp.int32))
+
+    def send(k):
+        far = z * half + lax.rem(me + k, half)
+        return far, pltpu.make_async_remote_copy(
+            src_ref=in_ref.at[far - z * half], dst_ref=land.at[me], send_sem=send_sem.at[k], recv_sem=recv_sem.at[me],
+            device_id=device(far), device_id_type=MESH,
+        )
+
+    def hand(s):
+        return pltpu.make_async_remote_copy(
+            src_ref=land.at[s], dst_ref=land.at[s], send_sem=out_sem.at[s], recv_sem=pass_sem.at[s],
+            device_id=sibling, device_id_type=MESH,
+        )
+
+    def start(k, unused):
+        far, copy = send(k)
+
+        @pl.when(far != me)
+        def _():
+            copy.start()
+
+        return unused
+
+    lax.fori_loop(0, half, start, 0)
+
+    @pl.when(owns)
+    def _():
+        land[me] = in_ref[me - z * half]
+        hand(me).start()
+
+        def take(k, unused):
+            s = lax.rem(me + k, tiles)
+            pltpu.make_async_remote_copy(
+                src_ref=in_ref.at[0], dst_ref=land.at[s], send_sem=send_sem.at[0], recv_sem=recv_sem.at[s],
+                device_id=device(s), device_id_type=MESH,
+            ).wait_recv()
+            hand(s).start()
+            return unused
+
+        lax.fori_loop(1, tiles, take, 0)
+
+        def sent(s, unused):
+            hand(s).wait_send()
+            return unused
+
+        lax.fori_loop(0, tiles, sent, 0)
+
+    @pl.when(jnp.logical_not(owns))
+    def _():
+        def got(s, unused):
+            hand(s).wait_recv()
+            return unused
+
+        lax.fori_loop(0, tiles, got, 0)
+
+    def finish(k, unused):
+        far, copy = send(k)
+
+        @pl.when(far != me)
+        def _():
+            copy.wait_send()
+
+        return unused
+
+    lax.fori_loop(0, half, finish, 0)
+    wide = -(-cap // 128) * 128
+    pieces = wide // 128
+    if out_ref.shape[1] > tiles * cap:
+        out_ref[...] = jnp.zeros(out_ref.shape, f32)
+    for s in range(tiles):
+        out_ref[0:8, s * cap : (s + 1) * cap] = land[s, :, 0:cap]
+        for i in range(3):
+            for j in range(pieces):
+                row = i * pieces + j
+                size = min(128, cap - j * 128)
+                out_ref[8 + i : 9 + i, s * cap + j * 128 : s * cap + j * 128 + size] = land[
+                    s, row % 8 : row % 8 + 1, wide + row // 8 * 128 : wide + row // 8 * 128 + size
+                ]
 
 
 def tap_weight(offset):
@@ -82,13 +201,9 @@
 
 
 def smear_kernel(
-    sources, cap, channels, levels, levels_all, wx, wy, in_ref, center_ref, xs_ref, ys_ref, cn_ref, rows_ref, a_ref, b_ref, h_ref, acc_ref, hacc_ref
+    sources, cap, channels, levels, levels_all, wx, wy, rows_ref, center_ref, xs_ref, ys_ref, cn_ref, a_ref, b_ref, h_ref, acc_ref, hacc_ref
 ):
     px = wx + 16
-    slots = sources * cap
-    rows_ref[...] = jnp.zeros(rows_ref.shape, f32)
-    for s in range(sources):
-        rows_ref[:, s * cap : (s + 1) * cap] = in_ref[s]
     first_level = lax.axis_index("gz") * levels
     acc_ref[...] = jnp.zeros(acc_ref.shape, f32)
     hacc_ref[...] = jnp.zeros(hacc_ref.shape, f32)
@@ -96,7 +211,7 @@
 
     def one(j, unused):
         lanes = pl.ds(pl.multiple_of(j * chunk, chunk), chunk)
-        cells = rows_ref[8:16, lanes].astype(jnp.int32)
+        cells = rows_ref[8:11, lanes].astype(jnp.int32)
         x, y, z = cells[0:1], cells[1:2], cells[2:3]
         gx = tap_weight(iota((px, chunk), 0) - reach - x)
         for c in range(channels):
@@ -178,6 +293,11 @@
             copy(i, dx, dy).wait_recv()
 
 
+def two(value, axis):
+    high = value.astype(bf16)
+    return jnp.concatenate([high, (value - high.astype(f32)).astype(bf16)], axis=axis)
+
+
 def state_kernel(nx, ny, base_ref, tend_ref, center_ref, rx_ref, ry_ref, rc_ref, out_ref):
     unused_g, x, y, unused_z = place()
     c = pl.program_id(0)
@@ -191,16 +311,15 @@
             size = corner.shape[1]
             row, col = iota((size, wx), 0), iota((size, wx), 1)
             put = ((row - c * 8 == col - end * (wx - 8)) & (row >= c * 8) & (row < c * 8 + 8)).astype(f32)
-            strip = strip + jnp.dot(corner, put, precision=lax.Precision.HIGHEST, preferred_element_type=f32)
+            strip = strip + jnp.dot(two(corner, 1), jnp.concatenate([put, put], axis=0).astype(bf16), preferred_element_type=f32)
         strips.append(strip)
     strip = jnp.concatenate(strips, axis=0)
     half = levels * 8
     row, col = iota((2 * half, levels * wy), 0), iota((2 * half, levels * wy), 1)
     side, level, cell = row // half, (row % half) // 8, row % 8
     put = (col == level * wy + cell + side * (wy - 8)).astype(f32)
-    source = center_ref[0] + lax.dot_general(
-        strip, put, (((0,), (0,)), ((), ())), precision=lax.Precision.HIGHEST, preferred_element_type=f32
-    )
+    put = jnp.concatenate([put, put], axis=0).astype(bf16)
+    source = center_ref[0] + lax.dot_general(two(strip, 0), put, (((0,), (0,)), ((), ())), preferred_element_type=f32)
     source = jnp.concatenate(
         [
             source[:8] + jnp.where(low_x, rx_ref[0, 0], 0.0),
@@ -328,20 +447,47 @@
     cap = max(2, (2 * points + tiles - 1) // tiles)
     channels, levels, wx, wy = base_state.shape
     px = wx + 16
-    forces = point_forces(inflow, chord_len, twist_base, compliance, blade_frame)
-    data = jnp.concatenate([forces, point_cells.astype(f32), jnp.zeros((5, points), f32)], axis=0)
+    half = tiles // nz
+    wide = -(-cap // 128) * 128
     slots = -(-tiles * cap // 512) * 512
+    message = wide + -(-3 * (wide // 128) // 8) * 128
     shape = jax.ShapeDtypeStruct
     packed = pl.pallas_call(
-        functools.partial(pack_kernel, tiles, cap),
-        out_shape=shape((tiles, 16, cap), f32),
-        in_specs=[VM, VM],
+        functools.partial(pack_kernel, tiles, cap, half),
+        out_shape=shape((half, 8, message), f32),
+        in_specs=[VM] * 7,
         out_specs=VM,
-        scratch_shapes=[pltpu.VMEM((1, points), jnp.int32), pltpu.VMEM((32, points), bf16), pltpu.VMEM((16, slots), f32)],
+        scratch_shapes=[
+            pltpu.VMEM((1, points), jnp.int32),
+            pltpu.VMEM((32, points), bf16),
+            pltpu.VMEM((16, -(-half * wide // 512) * 512), f32),
+        ],
         compiler_params=params(),
         name="pack_points",
-    )(data, owner_tile.reshape(1, points))
-    arrived = lax.all_to_all(packed, ("gx", "gy"), split_axis=0, concat_axis=0, tiled=True)
+    )(
+        inflow,
+        chord_len.reshape(1, points),
+        twist_base.reshape(1, points),
+        compliance.reshape(1, points),
+        blade_frame,
+        owner_tile.reshape(1, points),
+        point_cells,
+    )
+    arrived = pl.pallas_call(
+        functools.partial(points_kernel, tiles, cap, half, ny),
+        out_shape=shape((16, slots), f32),
+        in_specs=[VM],
+        out_specs=VM,
+        scratch_shapes=[
+            pltpu.VMEM((tiles, 8, message), f32),
+            pltpu.SemaphoreType.DMA((half,)),
+            pltpu.SemaphoreType.DMA((tiles,)),
+            pltpu.SemaphoreType.DMA((tiles,)),
+            pltpu.SemaphoreType.DMA((tiles,)),
+        ],
+        compiler_params=params(0),
+        name="exchange_points",
+    )(packed)
     chunk = 512
     center, xs, ys, cn = pl.pallas_call(
         functools.partial(smear_kernel, tiles, cap, channels, levels, levels * nz, wx, wy),
@@ -354,7 +500,6 @@
         in_specs=[VM],
         out_specs=(VM,) * 4,
         scratch_shapes=[
-            pltpu.VMEM((16, slots), f32),
             pltpu.VMEM((channels * px, chunk), bf16),
             pltpu.VMEM((levels * wy, chunk), bf16),
             pltpu.VMEM((levels * 16, chunk), bf16),

time: 65.3 us -> 57 us (0.87)
  blocking collectives: 18 us -> 0 us
  Pallas kernels: 38.9 us -> 47.2 us
  local copies, waits for them, and re-layouts: 2.87 us -> 8.57 us
  other arithmetic: 4.38 us -> 0 us
    all_to_all x1 -> x0, blocking collectives: 18 us -> none  [body(): lax.all_to_all(packed, ('gx', 'gy'), split_axis=0, concat_axis=0, tiled=T...]
    pallas_call x1 -> x2, Pallas kernels: 7.49 us -> 15.1 us  [the longest x1 10.8 us: body(): pl.pallas_call(functools.partial(points_kernel, tiles, cap, half, ny), ou...]
    unnamed x9 -> x15, local copies, waits for them, and re-layouts: 2.79 us -> 6.31 us
    reshape x0 -> x3, local copies, waits for them, and re-layouts: none -> 2.26 us  [the longest x1 0.83 us: body(): chord_len.reshape(1, points)]
    add x2 -> x0, other arithmetic: 2 us -> none  [the longest x1 1.06 us: point_forces(): speed_sq = normal * normal + tangent * tangent]
    mul x2 -> x0, other arithmetic: 1.52 us -> none  [the longest x1 0.81 us: point_forces(): lift_force = pressure * (2.0 * math.pi) * jnp.sin(attack)]
    pallas_call x1, Pallas kernels: 5.55 us -> 6.87 us  [body(): pl.pallas_call(functools.partial(rim_kernel, nx, ny), out_shape=(shape(xs...]
    pallas_call x1, Pallas kernels: 5.79 us -> 4.91 us  [body(): pl.pallas_call(functools.partial(state_kernel, nx, ny), grid=(channels,),...]
where the time goes in v2:
time: 57 us; the launch traced here: 56.5 us
  Pallas kernels  47.2 us (83%)
  local copies, waits for them, and re-layouts  8.57 us (15%)
  between operations  0.7 us (1%)
    pallas_call x1, Pallas kernels, body(): pl.pallas_call(functools.partial(points_kernel, tiles, cap, half, ny), ou...  10.8 us
    pallas_call x1, Pallas kernels, body(): pl.pallas_call(functools.partial(lines_kernel, nx, ny, nz), grid=(1,), ou...  10.7 us
    pallas_call x1, Pallas kernels, body(): pl.pallas_call(functools.partial(smear_kernel, tiles, cap, channels, leve...  9.6 us
    pallas_call x1, Pallas kernels, body(): pl.pallas_call(functools.partial(rim_kernel, nx, ny), out_shape=(shape(xs...  6.87 us
    unnamed x15, local copies, waits for them, and re-layouts  6.31 us
    pallas_call x1, Pallas kernels, body(): pl.pallas_call(functools.partial(state_kernel, nx, ny), grid=(channels,),...  4.91 us
    pallas_call x1, Pallas kernels, body(): pl.pallas_call(functools.partial(pack_kernel, tiles, cap, half), out_shap...  4.33 us

profile of v2, /device:TPU:0, one launch (start us, length us, event | category | flops | bytes accessed | tf_op | source)
XLA Modules:
  0.0 56.5 jit_solution(16101413851415325696)
XLA Ops:
  0.6 0.0 copy-start.1
  0.6 0.8 %reshape.16.chord_ref = f32[1,2304]{1,0:T(1,128)S(1)} reshape(f32[2304]{0:T(1024)} %param.12) | data formatting | bytes 18432 | tf_op jit(solution)/shard_map/reshape | solution.py:469
  1.5 0.7 %reshape.17.twist_ref = f32[1,2304]{1,0:T(1,128)S(1)} reshape(f32[2304]{0:T(1024)} %param.13) | data formatting | bytes 18432 | tf_op jit(solution)/shard_map/reshape | solution.py:470
  2.2 0.7 %reshape.18.compliance_ref = f32[1,2304]{1,0:T(1,128)S(1)} reshape(f32[2304]{0:T(1024)} %param.14) | data formatting | bytes 18432 | tf_op jit(solution)/shard_map/reshape | solution.py:471
  2.9 0.0 copy-start.3
  2.9 0.9 %copy-done.3 = f32[16,2304]{1,0:T(8,128)S(1)} copy-done((f32[16,2304]{1,0:T(8,128)S(1)}, f32[16,2304]{1,0:T(8,128)}, u32[]{:S(2)}) %copy-start.3) | copy-done | bytes 147480
  3.8 0.0 copy-start.4
  3.8 0.8 %copy-done.4 = s32[3,2304]{1,0:T(4,128)S(1)} copy-done((s32[3,2304]{1,0:T(4,128)S(1)}, s32[3,2304]{1,0:T(4,128)}, u32[]{:S(2)}) %copy-start.4) | copy-done | bytes 27672
  4.6 0.0 copy-start.5
  4.6 0.7 %copy-done.5 = f32[2,2304]{1,0:T(2,128)S(1)} copy-done((f32[2,2304]{1,0:T(2,128)S(1)}, f32[2,2304]{1,0:T(2,128)}, u32[]{:S(2)}) %copy-start.5) | copy-done | bytes 18456
  5.3 0.0 copy-start.6
  5.3 0.7 %copy-done.6 = s32[2304,1]{0,1:T(1,128)S(1)} copy-done((s32[2304,1]{0,1:T(1,128)S(1)}, s32[2304,1]{0,1:T(1,128)}, u32[]{:S(2)}) %copy-start.6) | copy-done | bytes 9240
  6.0 4.3 %pack_points.1.in_ref = f32[4,8,896]{2,1,0:T(8,128)S(1)} custom-call(f32[2,2304]{1,0:T(2,128)S(1)} %copy-done.5, f32[1,2304]{1,0:T(1,128)S(1)} %reshape.16.chord_ref, f32[1,2304]{1,0:T(1,128)S(1)} %reshape.17.twist_ref, f32[1,2304]{1,0:T(1,128)S(1)} %reshape.18.compliance_ref, f32[16,2304]{1,0:T(8,128)S(1)} %copy-done.3, s32[1,2304]{1,0:T(1,128)S(1)} %bitcast.1, ...), custom_call_target="tpu_custom_call" | custom-call | tf_op jit(solution)/shard_map/pack_points/pallas_call | solution.py:455
  10.3 10.8 %exchange_points.1.rows_ref = f32[16,4608]{1,0:T(8,128)S(1)} custom-call(f32[4,8,896]{2,1,0:T(8,128)S(1)} %pack_points.1.in_ref), custom_call_target="tpu_custom_call" | custom-call | tf_op jit(solution)/shard_map/exchange_points/pallas_call | solution.py:476
  21.2 9.6 %smear_points.1 = (f32[8,96,512]{2,1,0:T(8,128)S(1)}, f32[2,8,8,512]{3,2,1,0:T(8,128)S(1)}, f32[2,8,32,96]{3,2,1,0:T(8,128)S(1)}, f32[2,2,32,64]{3,2,1,0:T(8,128)S(1)}) custom-call(f32[16,4608]{1,0:T(8,128)S(1)} %exchange_points.1.rows_ref), custom_call_target="tpu_custom_call" | custom-call | tf_op jit(solution)/shard_map/smear_points/pallas_call | solution.py:492
  30.8 6.9 %exchange_rims.1 = (f32[2,8,8,512]{3,2,1,0:T(8,128)S(1)}, f32[2,8,32,96]{3,2,1,0:T(8,128)S(1)}, f32[2,2,32,64]{3,2,1,0:T(8,128)S(1)}) custom-call(f32[2,8,8,512]{3,2,1,0:T(8,128)S(1)} %get-tuple-element.10.xs_ref, f32[2,8,32,96]{3,2,1,0:T(8,128)S(1)} %get-tuple-element.11.ys_ref, f32[2,2,32,64]{3,2,1,0:T(8,128)S(1)} %get-tuple-element.12.cn_ref), custom_call_target="tpu_custom_call" | custom-call | tf_op jit(solution)/shard_map/exchange_rims/pallas_call | solution.py:512
  37.7 0.0 copy-done.1
  37.7 0.0 copy-start.2
  37.7 1.1 %copy-done.2 = bf16[8,4,96,128]{3,2,1,0:T(8,128)(2,1)S(1)} copy-done((bf16[8,4,96,128]{3,2,1,0:T(8,128)(2,1)S(1)}, bf16[8,4,96,128]{3,2,1,0:T(8,128)(2,1)}, u32[]{:S(2)}) %copy-start.2) | copy-done | bytes 786456
  38.8 4.9 %forced_state.1.fs_ref = f32[8,4,96,128]{3,2,1,0:T(8,128)} custom-call(f32[8,4,96,128]{3,2,1,0:T(8,128)S(1)} %copy-done.1, bf16[8,4,96,128]{3,2,1,0:T(8,128)(2,1)S(1)} %copy-done.2, f32[8,96,512]{2,1,0:T(8,128)S(1)} %get-tuple-element.9.center_ref, f32[2,8,8,512]{3,2,1,0:T(8,128)S(1)} %get-tuple-element.13.rx_ref, ...), custom_call_target="tpu_custom_call" | custom-call | tf_op jit(solution)/shard_map/forced_state/pallas_call | solution.py:521
  43.7 0.0 copy-start
  43.7 1.4 %copy-done = f32[8,4,96,128]{3,2,1,0:T(8,128)S(1)} copy-done((f32[8,4,96,128]{3,2,1,0:T(8,128)S(1)}, f32[8,4,96,128]{3,2,1,0:T(8,128)}, u32[]{:S(2)}) %copy-start) | copy-done | bytes 1572888
  45.1 10.7 %divergence_lines.1 = f32[4,32,384]{2,1,0:T(8,128)S(1)} custom-call(f32[8,4,96,128]{3,2,1,0:T(8,128)S(1)} %copy-done), custom_call_target="tpu_custom_call" | custom-call | tf_op jit(solution)/shard_map/divergence_lines/pallas_call | solution.py:538
  55.8 0.7 %copy.12 = f32[4,32,384]{2,1,0:T(8,128)} copy(f32[4,32,384]{2,1,0:T(8,128)S(1)} %divergence_lines.1) | data formatting | bytes 393216
Async XLA Ops:
  0.6 37.0 %copy-start.1 = (f32[8,4,96,128]{3,2,1,0:T(8,128)S(1)}, f32[8,4,96,128]{3,2,1,0:T(8,128)}, u32[]{:S(2)}) copy-start(f32[8,4,96,128]{3,2,1,0:T(8,128)} %base_ref.1) | copy-start | bytes 4718596
  2.9 0.9 %copy-start.3 = (f32[16,2304]{1,0:T(8,128)S(1)}, f32[16,2304]{1,0:T(8,128)}, u32[]{:S(2)}) copy-start(f32[16,2304]{1,0:T(8,128)} %frame_ref.1) | copy-start | bytes 442372
  3.8 0.8 %copy-start.4 = (s32[3,2304]{1,0:T(4,128)S(1)}, s32[3,2304]{1,0:T(4,128)}, u32[]{:S(2)}) copy-start(s32[3,2304]{1,0:T(4,128)} %cells_ref.1) | copy-start | bytes 82948
  4.6 0.7 %copy-start.5 = (f32[2,2304]{1,0:T(2,128)S(1)}, f32[2,2304]{1,0:T(2,128)}, u32[]{:S(2)}) copy-start(f32[2,2304]{1,0:T(2,128)} %inflow_ref.1) | copy-start | bytes 55300
  5.3 0.7 %copy-start.6 = (s32[2304,1]{0,1:T(1,128)S(1)}, s32[2304,1]{0,1:T(1,128)}, u32[]{:S(2)}) copy-start(s32[2304,1]{0,1:T(1,128)} %param.16) | copy-start | bytes 27652
  37.7 1.1 %copy-start.2 = (bf16[8,4,96,128]{3,2,1,0:T(8,128)(2,1)S(1)}, bf16[8,4,96,128]{3,2,1,0:T(8,128)(2,1)}, u32[]{:S(2)}) copy-start(bf16[8,4,96,128]{3,2,1,0:T(8,128)(2,1)} %tend_ref.1) | copy-start | bytes 2359300
  43.7 1.4 %copy-start = (f32[8,4,96,128]{3,2,1,0:T(8,128)S(1)}, f32[8,4,96,128]{3,2,1,0:T(8,128)}, u32[]{:S(2)}) copy-start(f32[8,4,96,128]{3,2,1,0:T(8,128)} %forced_state.1.fs_ref) | copy-start | bytes 4718596

commit v3 on v2

--- a/solution.py
+++ b/solution.py
@@ -16,6 +16,7 @@
 VM = pl.BlockSpec(memory_space=pltpu.VMEM)
 ANY = pl.BlockSpec(memory_space=pl.ANY)
 LIMIT = 48 * 1024 * 1024
+WIDE = 58 * 1024 * 1024
 f32 = jnp.float32
 bf16 = jnp.bfloat16
 
@@ -36,6 +37,10 @@
     poly = ((8.05374449538e-2 * q - 1.38776856032e-1) * q + 1.99777106478e-1) * q - 3.33329491539e-1
     angle = jnp.where(upper, math.pi / 4, 0.0) + (poly * q * r + r)
     return jnp.where(n > t, math.pi / 2 - angle, angle)
+
+
+def flat(ref):
+    return ref[...].reshape(1, ref.shape[0])
 
 
 def pack_kernel(
@@ -56,8 +61,8 @@
         slot_ref[:, k * step : (k + 1) * step] = position.astype(jnp.int32) + (here - mine) * wide
     normal, tangent = inflow_ref[0:1, :], inflow_ref[1:2, :]
     speed_sq = normal * normal + tangent * tangent
-    attack = arc_tangent(normal, tangent) - (twist_ref[...] + compliance_ref[...] * speed_sq)
-    pressure = 0.5 * speed_sq * chord_ref[...]
+    attack = arc_tangent(normal, tangent) - (flat(twist_ref) + flat(compliance_ref) * speed_sq)
+    pressure = 0.5 * speed_sq * flat(chord_ref)
     lift = pressure * (2.0 * math.pi) * jnp.sin(attack)
     drag = pressure * (0.01 + 0.5 * attack * attack)
     channels = frame_ref.shape[0] // 2
@@ -94,7 +99,7 @@
                 ]
 
 
-def points_kernel(tiles, cap, half, ny, in_ref, out_ref, land, send_sem, recv_sem, out_sem, pass_sem):
+def points_kernel(tiles, cap, half, ny, in_ref, out_ref, land, send_sem, recv_sem, out_sem, pass_sem, own_sem):
     g, x, y, z = place()
     me = x * ny + y
     owns = me // half == z
@@ -142,7 +147,9 @@
 
     @pl.when(owns)
     def _():
-        land[me] = in_ref[me - z * half]
+        own = pltpu.make_async_copy(in_ref.at[me - z * half], land.at[me], own_sem)
+        own.start()
+        own.wait()
         hand(me).start()
 
         def take(k, unused):
@@ -207,29 +214,43 @@
     first_level = lax.axis_index("gz") * levels
     acc_ref[...] = jnp.zeros(acc_ref.shape, f32)
     hacc_ref[...] = jnp.zeros(hacc_ref.shape, f32)
-    chunk = a_ref.shape[1]
-
-    def one(j, unused):
+    folds, chunk = a_ref.shape[0], a_ref.shape[2]
+
+    def fill(j, i):
         lanes = pl.ds(pl.multiple_of(j * chunk, chunk), chunk)
         cells = rows_ref[8:11, lanes].astype(jnp.int32)
         x, y, z = cells[0:1], cells[1:2], cells[2:3]
         gx = tap_weight(iota((px, chunk), 0) - reach - x)
         for c in range(channels):
-            a_ref[c * px : (c + 1) * px, :] = (rows_ref[c : c + 1, lanes] * gx).astype(bf16)
+            a_ref[i, c * px : (c + 1) * px, :] = (rows_ref[c : c + 1, lanes] * gx).astype(bf16)
         every = (iota((levels_all, chunk), 0) - z).astype(f32) * (1.0 / sigma_z)
         total = 1.0 / jnp.sum(jnp.exp(-every * every), axis=0, keepdims=True)
         gy = tap_weight(iota((wy + 16, chunk), 0) - reach - y).astype(bf16).astype(f32)
         for k in range(levels):
             near = (first_level + k - z).astype(f32) * (1.0 / sigma_z)
             gz = jnp.exp(-near * near) * total
-            b_ref[k * wy : (k + 1) * wy, :] = (gy[8 : 8 + wy] * gz).astype(bf16)
+            b_ref[i, k * wy : (k + 1) * wy, :] = (gy[8 : 8 + wy] * gz).astype(bf16)
             rims = jnp.concatenate([gy[0:8] * gz, gy[8 + wy :] * gz], axis=0)
-            h_ref[k * 16 : (k + 1) * 16, :] = rims.astype(bf16)
-        acc_ref[...] += dot_nt(a_ref[...], b_ref[...])
-        hacc_ref[...] += dot_nt(h_ref[...], a_ref[...])
+            h_ref[i, k * 16 : (k + 1) * 16, :] = rims.astype(bf16)
+
+    def add(i):
+        acc_ref[...] += dot_nt(a_ref[i], b_ref[i])
+        hacc_ref[...] += dot_nt(h_ref[i], a_ref[i])
+
+    count = rows_ref.shape[1] // chunk
+    fill(0, 0)
+
+    def one(j, unused):
+        for i in range(folds):
+            fill(jnp.minimum(j * folds + i + 1, count - 1), (i + 1) % folds)
+            add(i)
         return unused
 
-    lax.fori_loop(0, rows_ref.shape[1] // chunk, one, 0)
+    lax.fori_loop(0, count // folds, one, 0)
+    for i in range(count % folds):
+        if i + 1 < count % folds:
+            fill(count - count % folds + i + 1, i + 1)
+        add(i)
     for c in range(channels):
         center_ref[c] = acc_ref[c * px + 8 : c * px + 8 + wx, :]
         xs_ref[0, c] = acc_ref[c * px : c * px + 8, :]
@@ -298,7 +319,7 @@
     return jnp.concatenate([high, (value - high.astype(f32)).astype(bf16)], axis=axis)
 
 
-def state_kernel(nx, ny, base_ref, tend_ref, center_ref, rx_ref, ry_ref, rc_ref, out_ref):
+def state_kernel(nx, ny, base_ref, tend_ref, center_ref, rx_ref, ry_ref, rc_ref, out_ref, uvw_ref, put_ref):
     unused_g, x, y, unused_z = place()
     c = pl.program_id(0)
     levels, wx, wy = base_ref.shape[1:]
@@ -315,11 +336,15 @@
         strips.append(strip)
     strip = jnp.concatenate(strips, axis=0)
     half = levels * 8
-    row, col = iota((2 * half, levels * wy), 0), iota((2 * half, levels * wy), 1)
-    side, level, cell = row // half, (row % half) // 8, row % 8
-    put = (col == level * wy + cell + side * (wy - 8)).astype(f32)
-    put = jnp.concatenate([put, put], axis=0).astype(bf16)
-    source = center_ref[0] + lax.dot_general(two(strip, 0), put, (((0,), (0,)), ((), ())), preferred_element_type=f32)
+
+    @pl.when(c == 0)
+    def _():
+        row, col = iota((2 * half, levels * wy), 0), iota((2 * half, levels * wy), 1)
+        side, level, cell = row // half, (row % half) // 8, row % 8
+        put = (col == level * wy + cell + side * (wy - 8)).astype(f32)
+        put_ref[...] = jnp.concatenate([put, put], axis=0).astype(bf16)
+
+    source = center_ref[0] + lax.dot_general(two(strip, 0), put_ref[...], (((0,), (0,)), ((), ())), preferred_element_type=f32)
     source = jnp.concatenate(
         [
             source[:8] + jnp.where(low_x, rx_ref[0, 0], 0.0),
@@ -329,7 +354,12 @@
         axis=0,
     )
     for k in range(levels):
-        out_ref[0, k] = base_ref[0, k] + 0.5 * (tend_ref[0, k].astype(f32) + source[:, k * wy : (k + 1) * wy])
+        value = base_ref[0, k] + 0.5 * (tend_ref[0, k].astype(f32) + source[:, k * wy : (k + 1) * wy])
+        out_ref[0, k] = value
+
+        @pl.when(c < 3)
+        def _():
+            uvw_ref[jnp.minimum(c, 2), k] = value
 
 
 def lines_kernel(nx, ny, nz, fs_ref, out_ref, su, sv, ru, rv, rw, lines, land, hs, hr, ls, lr):
@@ -434,9 +464,9 @@
         out_ref[:, :, j * wx : (j + 1) * wx] = land[j]
 
 
-def params(collective_id=None):
+def params(collective_id=None, limit=LIMIT):
     if collective_id is None:
-        return pltpu.CompilerParams(vmem_limit_bytes=LIMIT)
+        return pltpu.CompilerParams(vmem_limit_bytes=limit)
     return pltpu.CompilerParams(vmem_limit_bytes=LIMIT, collective_id=collective_id, has_side_effects=True)
 
 
@@ -455,20 +485,29 @@
     packed = pl.pallas_call(
         functools.partial(pack_kernel, tiles, cap, half),
         out_shape=shape((half, 8, message), f32),
-        in_specs=[VM] * 7,
+        grid=(1,),
+        in_specs=[
+            pl.BlockSpec((2, points), lambda i: (0, 0)),
+            pl.BlockSpec((points,), lambda i: (0,)),
+            pl.BlockSpec((points,), lambda i: (0,)),
+            pl.BlockSpec((points,), lambda i: (0,)),
+            pl.BlockSpec(blade_frame.shape, lambda i: (0, 0)),
+            pl.BlockSpec((1, points), lambda i: (0, 0)),
+            pl.BlockSpec(point_cells.shape, lambda i: (0, 0)),
+        ],
         out_specs=VM,
         scratch_shapes=[
             pltpu.VMEM((1, points), jnp.int32),
             pltpu.VMEM((32, points), bf16),
             pltpu.VMEM((16, -(-half * wide // 512) * 512), f32),
         ],
-        compiler_params=params(),
+        compiler_params=params(limit=WIDE),
         name="pack_points",
     )(
         inflow,
-        chord_len.reshape(1, points),
-        twist_base.reshape(1, points),
-        compliance.reshape(1, points),
+        chord_len,
+        twist_base,
+        compliance,
         blade_frame,
         owner_tile.reshape(1, points),
         point_cells,
@@ -476,7 +515,7 @@
     arrived = pl.pallas_call(
         functools.partial(points_kernel, tiles, cap, half, ny),
         out_shape=shape((16, slots), f32),
-        in_specs=[VM],
+        in_specs=[ANY],
         out_specs=VM,
         scratch_shapes=[
             pltpu.VMEM((tiles, 8, message), f32),
@@ -484,6 +523,7 @@
             pltpu.SemaphoreType.DMA((tiles,)),
             pltpu.SemaphoreType.DMA((tiles,)),
             pltpu.SemaphoreType.DMA((tiles,)),
+            pltpu.SemaphoreType.DMA,
         ],
         compiler_params=params(0),
         name="exchange_points",
@@ -500,9 +540,9 @@
         in_specs=[VM],
         out_specs=(VM,) * 4,
         scratch_shapes=[
-            pltpu.VMEM((channels * px, chunk), bf16),
-            pltpu.VMEM((levels * wy, chunk), bf16),
-            pltpu.VMEM((levels * 16, chunk), bf16),
+            pltpu.VMEM((2, channels * px, chunk), bf16),
+            pltpu.VMEM((2, levels * wy, chunk), bf16),
+            pltpu.VMEM((2, levels * 16, chunk), bf16),
             pltpu.VMEM((channels * px, levels * wy), f32),
             pltpu.VMEM((levels * 16, channels * px), f32),
         ],
@@ -518,10 +558,10 @@
         compiler_params=params(1),
         name="exchange_rims",
     )(xs, ys, cn)
-    forced_state = pl.pallas_call(
+    forced_state, velocity = pl.pallas_call(
         functools.partial(state_kernel, nx, ny),
         grid=(channels,),
-        out_shape=shape(base_state.shape, f32),
+        out_shape=(shape(base_state.shape, f32), shape((3, levels, wx, wy), f32)),
         in_specs=[
             pl.BlockSpec((1, levels, wx, wy), lambda c: (c, 0, 0, 0)),
             pl.BlockSpec((1, levels, wx, wy), lambda c: (c, 0, 0, 0)),
@@ -530,17 +570,17 @@
             pl.BlockSpec((2, 1, levels * 8, wx), lambda c: (0, c, 0, 0)),
             pl.BlockSpec(cn.shape, lambda c: (0, 0, 0, 0)),
         ],
-        out_specs=pl.BlockSpec((1, levels, wx, wy), lambda c: (c, 0, 0, 0)),
+        out_specs=(pl.BlockSpec((1, levels, wx, wy), lambda c: (c, 0, 0, 0)), VM),
+        scratch_shapes=[pltpu.VMEM((4 * levels * 8, levels * wy), bf16)],
         compiler_params=params(),
         name="forced_state",
     )(base_state, tendency, center, rx, ry, rc)
     band = wy // nx
     divergence_lines = pl.pallas_call(
         functools.partial(lines_kernel, nx, ny, nz),
-        grid=(1,),
         out_shape=shape((levels, band, nx * wx), f32),
-        in_specs=[pl.BlockSpec((3, levels, wx, wy), lambda i: (0, 0, 0, 0))],
-        out_specs=pl.BlockSpec((levels, band, nx * wx), lambda i: (0, 0, 0)),
+        in_specs=[VM],
+        out_specs=VM,
         scratch_shapes=[
             pltpu.VMEM((2, levels, wy), f32),
             pltpu.VMEM((2, levels, wx), f32),
@@ -556,7 +596,7 @@
         ],
         compiler_params=params(2),
         name="divergence_lines",
-    )(forced_state)
+    )(velocity)
     return (forced_state, divergence_lines)
 
 

time: 57 us -> 51.6 us (0.905)
  local copies, waits for them, and re-layouts: 8.57 us -> 2.71 us
  Pallas kernels: 47.2 us -> 48 us
    unnamed x15 -> x7, local copies, waits for them, and re-layouts: 6.31 us -> 2.71 us
    reshape x3 -> x0, local copies, waits for them, and re-layouts: 2.26 us -> none  [the longest x1 0.83 us: body(): chord_len.reshape(1, points)]
    pallas_call x1, Pallas kernels: 4.33 us -> 6.09 us  [body(): pl.pallas_call(functools.partial(pack_kernel, tiles, cap, half), out_shap...]
    pallas_call x1, Pallas kernels: 9.6 us -> 8.48 us  [body(): pl.pallas_call(functools.partial(smear_kernel, tiles, cap, channels, leve...]
where the time goes in v3:
time: 51.6 us; the launch traced here: 51.4 us
  Pallas kernels  48 us (93%)
  local copies, waits for them, and re-layouts  2.71 us (5%)
  between operations  0.69 us (1%)
    pallas_call x1, Pallas kernels, body(): pl.pallas_call(functools.partial(points_kernel, tiles, cap, half, ny), ou...  10.8 us
    pallas_call x1, Pallas kernels, body(): pl.pallas_call(functools.partial(lines_kernel, nx, ny, nz), out_shape=sha...  10.7 us
    pallas_call x1, Pallas kernels, body(): pl.pallas_call(functools.partial(smear_kernel, tiles, cap, channels, leve...  8.48 us
    pallas_call x1, Pallas kernels, body(): pl.pallas_call(functools.partial(rim_kernel, nx, ny), out_shape=(shape(xs...  6.86 us
    pallas_call x1, Pallas kernels, body(): pl.pallas_call(functools.partial(pack_kernel, tiles, cap, half), out_shap...  6.09 us
    pallas_call x1, Pallas kernels, body(): pl.pallas_call(functools.partial(state_kernel, nx, ny), grid=(channels,),...  5.09 us
    unnamed x7, local copies, waits for them, and re-layouts  2.71 us

profile of v3, /device:TPU:0, one launch (start us, length us, event | category | flops | bytes accessed | tf_op | source)
XLA Modules:
  0.0 51.4 jit_solution(10060962813879760356)
XLA Ops:
  0.6 0.0 copy-start
  0.6 6.1 %pack_points.1.in_ref = f32[4,8,896]{2,1,0:T(8,128)} custom-call(f32[2,2304]{1,0:T(2,128)} %inflow_ref.1, f32[2304]{0:T(1024)} %chord_ref.1, f32[2304]{0:T(1024)} %twist_ref.1, f32[2304]{0:T(1024)} %compliance_ref.1, f32[16,2304]{1,0:T(8,128)} %frame_ref.1, s32[1,2304]{1,0:T(1,128)} %bitcast.1, s32[3,2304]{1,0:T(4,128)} %cells_ref.1), custom_call_target="tpu_custom_call" | custom-call | tf_op jit(solution)/shard_map/pack_points/pallas_call | solution.py:485
  6.7 0.0 copy-start.2
  6.7 0.9 %copy-done.2 = f32[4,8,896]{2,1,0:T(8,128)S(1)} copy-done((f32[4,8,896]{2,1,0:T(8,128)S(1)}, f32[4,8,896]{2,1,0:T(8,128)}, u32[]{:S(2)}) %copy-start.2) | copy-done | bytes 114712
  7.6 10.8 %exchange_points.1.rows_ref = f32[16,4608]{1,0:T(8,128)S(1)} custom-call(f32[4,8,896]{2,1,0:T(8,128)S(1)} %copy-done.2), custom_call_target="tpu_custom_call" | custom-call | tf_op jit(solution)/shard_map/exchange_points/pallas_call | solution.py:515
  18.4 8.5 %smear_points.1 = (f32[8,96,512]{2,1,0:T(8,128)S(1)}, f32[2,8,8,512]{3,2,1,0:T(8,128)S(1)}, f32[2,8,32,96]{3,2,1,0:T(8,128)S(1)}, f32[2,2,32,64]{3,2,1,0:T(8,128)S(1)}) custom-call(f32[16,4608]{1,0:T(8,128)S(1)} %exchange_points.1.rows_ref), custom_call_target="tpu_custom_call" | custom-call | tf_op jit(solution)/shard_map/smear_points/pallas_call | solution.py:532
  26.9 6.9 %exchange_rims.1 = (f32[2,8,8,512]{3,2,1,0:T(8,128)S(1)}, f32[2,8,32,96]{3,2,1,0:T(8,128)S(1)}, f32[2,2,32,64]{3,2,1,0:T(8,128)S(1)}) custom-call(f32[2,8,8,512]{3,2,1,0:T(8,128)S(1)} %get-tuple-element.12.xs_ref, f32[2,8,32,96]{3,2,1,0:T(8,128)S(1)} %get-tuple-element.13.ys_ref, f32[2,2,32,64]{3,2,1,0:T(8,128)S(1)} %get-tuple-element.14.cn_ref), custom_call_target="tpu_custom_call" | custom-call | tf_op jit(solution)/shard_map/exchange_rims/pallas_call | solution.py:552
  33.7 0.0 copy-done
  33.8 0.0 copy-start.1
  33.8 1.1 %copy-done.1 = bf16[8,4,96,128]{3,2,1,0:T(8,128)(2,1)S(1)} copy-done((bf16[8,4,96,128]{3,2,1,0:T(8,128)(2,1)S(1)}, bf16[8,4,96,128]{3,2,1,0:T(8,128)(2,1)}, u32[]{:S(2)}) %copy-start.1) | copy-done | bytes 786456
  34.9 5.1 %forced_state.1 = (f32[8,4,96,128]{3,2,1,0:T(8,128)}, f32[3,4,96,128]{3,2,1,0:T(8,128)S(1)}) custom-call(f32[8,4,96,128]{3,2,1,0:T(8,128)S(1)} %copy-done, bf16[8,4,96,128]{3,2,1,0:T(8,128)(2,1)S(1)} %copy-done.1, f32[8,96,512]{2,1,0:T(8,128)S(1)} %get-tuple-element.11.center_ref, f32[2,8,8,512]{3,2,1,0:T(8,128)S(1)} %get-tuple-element.15.rx_ref, ...), custom_call_target="tpu_custom_call" | custom-call | tf_op jit(solution)/shard_map/forced_state/pallas_call | solution.py:561
  40.0 10.7 %divergence_lines.1 = f32[4,32,384]{2,1,0:T(8,128)S(1)} custom-call(f32[3,4,96,128]{3,2,1,0:T(8,128)S(1)} %get-tuple-element.19.fs_ref), custom_call_target="tpu_custom_call" | custom-call | tf_op jit(solution)/shard_map/divergence_lines/pallas_call | solution.py:579
  50.7 0.7 %copy.12 = f32[4,32,384]{2,1,0:T(8,128)} copy(f32[4,32,384]{2,1,0:T(8,128)S(1)} %divergence_lines.1) | data formatting | bytes 393216
Async XLA Ops:
  0.6 33.1 %copy-start = (f32[8,4,96,128]{3,2,1,0:T(8,128)S(1)}, f32[8,4,96,128]{3,2,1,0:T(8,128)}, u32[]{:S(2)}) copy-start(f32[8,4,96,128]{3,2,1,0:T(8,128)} %base_ref.1) | copy-start | bytes 4718596
  6.7 0.9 %copy-start.2 = (f32[4,8,896]{2,1,0:T(8,128)S(1)}, f32[4,8,896]{2,1,0:T(8,128)}, u32[]{:S(2)}) copy-start(f32[4,8,896]{2,1,0:T(8,128)} %pack_points.1.in_ref) | copy-start | bytes 344068
  33.8 1.1 %copy-start.1 = (bf16[8,4,96,128]{3,2,1,0:T(8,128)(2,1)S(1)}, bf16[8,4,96,128]{3,2,1,0:T(8,128)(2,1)}, u32[]{:S(2)}) copy-start(bf16[8,4,96,128]{3,2,1,0:T(8,128)(2,1)} %tend_ref.1) | copy-start | bytes 2359300

commit v4 on v3

--- a/solution.py
+++ b/solution.py
@@ -479,7 +479,7 @@
     px = wx + 16
     half = tiles // nz
     wide = -(-cap // 128) * 128
-    slots = -(-tiles * cap // 512) * 512
+    slots = -(-tiles * cap // 768) * 768
     message = wide + -(-3 * (wide // 128) // 8) * 128
     shape = jax.ShapeDtypeStruct
     packed = pl.pallas_call(
@@ -528,7 +528,7 @@
         compiler_params=params(0),
         name="exchange_points",
     )(packed)
-    chunk = 512
+    chunk = 768
     center, xs, ys, cn = pl.pallas_call(
         functools.partial(smear_kernel, tiles, cap, channels, levels, levels * nz, wx, wy),
         out_shape=(

time: 51.6 us -> 51.6 us (level)
  no operation moved by 1% of the time
where the time goes in v4:
time: 51.6 us; the launch traced here: 51.4 us
  Pallas kernels  48 us (93%)
  local copies, waits for them, and re-layouts  2.71 us (5%)
  between operations  0.69 us (1%)
    pallas_call x1, Pallas kernels, body(): pl.pallas_call(functools.partial(points_kernel, tiles, cap, half, ny), ou...  10.8 us
    pallas_call x1, Pallas kernels, body(): pl.pallas_call(functools.partial(lines_kernel, nx, ny, nz), out_shape=sha...  10.7 us
    pallas_call x1, Pallas kernels, body(): pl.pallas_call(functools.partial(smear_kernel, tiles, cap, channels, leve...  8.54 us
    pallas_call x1, Pallas kernels, body(): pl.pallas_call(functools.partial(rim_kernel, nx, ny), out_shape=(shape(xs...  6.86 us
    pallas_call x1, Pallas kernels, body(): pl.pallas_call(functools.partial(pack_kernel, tiles, cap, half), out_shap...  6.09 us
    pallas_call x1, Pallas kernels, body(): pl.pallas_call(functools.partial(state_kernel, nx, ny), grid=(channels,),...  5.09 us
    unnamed x7, local copies, waits for them, and re-layouts  2.71 us

profile of v4, /device:TPU:0, one launch (start us, length us, event | category | flops | bytes accessed | tf_op | source)
XLA Modules:
  0.0 51.4 jit_solution(18180476222076612412)
XLA Ops:
  0.6 0.0 copy-start
  0.6 6.1 %pack_points.1.in_ref = f32[4,8,896]{2,1,0:T(8,128)} custom-call(f32[2,2304]{1,0:T(2,128)} %inflow_ref.1, f32[2304]{0:T(1024)} %chord_ref.1, f32[2304]{0:T(1024)} %twist_ref.1, f32[2304]{0:T(1024)} %compliance_ref.1, f32[16,2304]{1,0:T(8,128)} %frame_ref.1, s32[1,2304]{1,0:T(1,128)} %bitcast.1, s32[3,2304]{1,0:T(4,128)} %cells_ref.1), custom_call_target="tpu_custom_call" | custom-call | tf_op jit(solution)/shard_map/pack_points/pallas_call | solution.py:485
  6.7 0.0 copy-start.2
  6.7 0.9 %copy-done.2 = f32[4,8,896]{2,1,0:T(8,128)S(1)} copy-done((f32[4,8,896]{2,1,0:T(8,128)S(1)}, f32[4,8,896]{2,1,0:T(8,128)}, u32[]{:S(2)}) %copy-start.2) | copy-done | bytes 114712
  7.6 10.8 %exchange_points.1.rows_ref = f32[16,4608]{1,0:T(8,128)S(1)} custom-call(f32[4,8,896]{2,1,0:T(8,128)S(1)} %copy-done.2), custom_call_target="tpu_custom_call" | custom-call | tf_op jit(solution)/shard_map/exchange_points/pallas_call | solution.py:515
  18.4 8.5 %smear_points.1 = (f32[8,96,512]{2,1,0:T(8,128)S(1)}, f32[2,8,8,512]{3,2,1,0:T(8,128)S(1)}, f32[2,8,32,96]{3,2,1,0:T(8,128)S(1)}, f32[2,2,32,64]{3,2,1,0:T(8,128)S(1)}) custom-call(f32[16,4608]{1,0:T(8,128)S(1)} %exchange_points.1.rows_ref), custom_call_target="tpu_custom_call" | custom-call | tf_op jit(solution)/shard_map/smear_points/pallas_call | solution.py:532
  26.9 6.9 %exchange_rims.1 = (f32[2,8,8,512]{3,2,1,0:T(8,128)S(1)}, f32[2,8,32,96]{3,2,1,0:T(8,128)S(1)}, f32[2,2,32,64]{3,2,1,0:T(8,128)S(1)}) custom-call(f32[2,8,8,512]{3,2,1,0:T(8,128)S(1)} %get-tuple-element.12.xs_ref, f32[2,8,32,96]{3,2,1,0:T(8,128)S(1)} %get-tuple-element.13.ys_ref, f32[2,2,32,64]{3,2,1,0:T(8,128)S(1)} %get-tuple-element.14.cn_ref), custom_call_target="tpu_custom_call" | custom-call | tf_op jit(solution)/shard_map/exchange_rims/pallas_call | solution.py:552
  33.8 0.0 copy-done
  33.8 0.0 copy-start.1
  33.8 1.1 %copy-done.1 = bf16[8,4,96,128]{3,2,1,0:T(8,128)(2,1)S(1)} copy-done((bf16[8,4,96,128]{3,2,1,0:T(8,128)(2,1)S(1)}, bf16[8,4,96,128]{3,2,1,0:T(8,128)(2,1)}, u32[]{:S(2)}) %copy-start.1) | copy-done | bytes 786456
  35.0 5.1 %forced_state.1 = (f32[8,4,96,128]{3,2,1,0:T(8,128)}, f32[3,4,96,128]{3,2,1,0:T(8,128)S(1)}) custom-call(f32[8,4,96,128]{3,2,1,0:T(8,128)S(1)} %copy-done, bf16[8,4,96,128]{3,2,1,0:T(8,128)(2,1)S(1)} %copy-done.1, f32[8,96,512]{2,1,0:T(8,128)S(1)} %get-tuple-element.11.center_ref, f32[2,8,8,512]{3,2,1,0:T(8,128)S(1)} %get-tuple-element.15.rx_ref, ...), custom_call_target="tpu_custom_call" | custom-call | tf_op jit(solution)/shard_map/forced_state/pallas_call | solution.py:561
  40.0 10.7 %divergence_lines.1 = f32[4,32,384]{2,1,0:T(8,128)S(1)} custom-call(f32[3,4,96,128]{3,2,1,0:T(8,128)S(1)} %get-tuple-element.19.fs_ref), custom_call_target="tpu_custom_call" | custom-call | tf_op jit(solution)/shard_map/divergence_lines/pallas_call | solution.py:579
  50.7 0.7 %copy.12 = f32[4,32,384]{2,1,0:T(8,128)} copy(f32[4,32,384]{2,1,0:T(8,128)S(1)} %divergence_lines.1) | data formatting | bytes 393216
Async XLA Ops:
  0.6 33.2 %copy-start = (f32[8,4,96,128]{3,2,1,0:T(8,128)S(1)}, f32[8,4,96,128]{3,2,1,0:T(8,128)}, u32[]{:S(2)}) copy-start(f32[8,4,96,128]{3,2,1,0:T(8,128)} %base_ref.1) | copy-start | bytes 4718596
  6.7 0.9 %copy-start.2 = (f32[4,8,896]{2,1,0:T(8,128)S(1)}, f32[4,8,896]{2,1,0:T(8,128)}, u32[]{:S(2)}) copy-start(f32[4,8,896]{2,1,0:T(8,128)} %pack_points.1.in_ref) | copy-start | bytes 344068
  33.8 1.1 %copy-start.1 = (bf16[8,4,96,128]{3,2,1,0:T(8,128)(2,1)S(1)}, bf16[8,4,96,128]{3,2,1,0:T(8,128)(2,1)}, u32[]{:S(2)}) copy-start(bf16[8,4,96,128]{3,2,1,0:T(8,128)(2,1)} %tend_ref.1) | copy-start | bytes 2359300
